TPU v7x, 768 devices: a whole 4x8x12 slice. The times are simulated.
768 devices in a mesh: rep: 16 (over y, core), grp: 48 (over z, x).
Axes of the slice: x: 4, y: 8, z: 12, core: 2. Of those that a mesh axis runs over, the one named last changes fastest.
Arguments:
- grad_terms: bfloat16 [16, 48, 384, 4096], P('rep', 'grp'), may hold values from -5 to 5
- error_buffer: float32 [16, 384, 4096], P('rep', 'grp'), may hold values from -6 to 6
- weight: float32 [384, 4096], P('grp'), may hold values from -6 to 6
- q_prev: float32 [4096, 64], replicated, may hold values from -0.09375 to 0.09375
Outputs:
- q_next: float32 [4096, 64], replicated
- error_next: float32 [16, 384, 4096], P('rep', 'grp')
- weight_next: float32 [384, 4096], P('grp')
All inputs are finite; a program needn't handle non-finite values.
Results may differ from a plain program's by a relative error of at most 0.0003.
Values sent between devices are 32-bit elements; how exact they have to be, the bound alone decides.
No kernel may reach another device: no remote copies, remote signals or barrier semaphores. Data moves between devices by JAX's collectives and lax.ppermute only.
A program may use at most 32 MiB of HBM per device.

v0:
```python
import jax
import jax.numpy as jnp
from jax import lax
from jax.sharding import PartitionSpec as P


def full_dot(left, right):
    return jnp.dot(left, right, precision=lax.Precision.HIGHEST)


def on_device(grad_terms, error_buffer, weight, q_prev):
    term = grad_terms[0, 0].astype(jnp.float32)
    summed = lax.psum_scatter(term, "grp", scatter_dimension=0, tiled=True)
    corrected = summed + error_buffer[0]
    groups = lax.axis_size("rep")
    rank = q_prev.shape[1]
    left = lax.psum(full_dot(corrected, q_prev), "rep")
    gram = lax.psum(full_dot(left.T, left), "grp")
    shift = 0.01 * (jnp.trace(gram) / rank + 1e-06)
    shifted = gram + shift * jnp.eye(rank, dtype=gram.dtype)
    lower = jnp.linalg.cholesky(shifted)
    left_hat = lax.linalg.triangular_solve(
        lower, left, left_side=False, lower=True, transpose_a=True
    )
    q_next = lax.psum(full_dot(corrected.T, left_hat), ("rep", "grp")) / groups
    approx = full_dot(left_hat, q_next.T)
    error_next = (corrected - approx)[None]
    weight_next = weight - 0.5 * approx
    return (q_next, error_next, weight_next)


def solution(mesh):
    placed = (P("rep", "grp", None, None), P("rep", "grp", None), P("grp", None), P())
    return jax.shard_map(
        on_device,
        mesh=mesh,
        in_specs=placed,
        out_specs=(P(), P("rep", "grp", None), P("grp", None)),
        check_vma=False,
    )
```

profile of v0, /device:TPU:6, one launch (start us, length us, event | category | flops | bytes accessed | tf_op | source)
XLA Modules:
  0.0 1186.3 jit_solution(13990850338952775952)
XLA Ops:
  7.2 0.0 copy-start
  7.2 0.0 copy-start.2
  7.2 0.0 reduce-scatter.2.cloned.1.call-start
  7.2 5.4 bitcast_convert_fusion
  12.6 0.0 copy-start.4
  12.6 0.0 reduce-scatter.2.cloned.1.call-update
  12.7 0.0 all-reduce.2.cloned.1.call-start
  12.7 448.9 %reduce-scatter.2.cloned.1.call-done = f32[8,4096]{1,0:T(8,128)} async-done(((f32[384,4096]{1,0:T(8,128)}), f32[8,4096]{1,0:T(8,128)}) %reduce-scatter.2.cloned.1.call-update) | async-done | bytes 131088 | tf_op jit(solution)/shard_map/reduce_scatter | solution.py:13
  461.6 0.0 copy-done
  461.6 0.0 copy-done.2
  461.6 0.0 copy-start.3
  461.6 1.9 fusion.5
  463.5 23.6 %psum.21 = f32[8,64]{1,0:T(8,128)S(1)} all-reduce(f32[8,64]{1,0:T(8,128)S(1)} %fusion.5), channel_id=1, replica_groups=mesh['rep'=16,'grp'=48] {'rep'}, use_global_device_ids=true, to_apply=%region_1.0 | all-reduce | flops 512 | bytes 4096 | tf_op jit(solution)/shard_map/psum | solution.py:17
  487.1 0.2 fusion.6
  487.3 200.2 %psum.22 = f32[64,64]{1,0:T(8,128)S(1)} all-reduce(f32[64,64]{1,0:T(8,128)S(1)} %fusion.6), channel_id=1, replica_groups=mesh['rep'=16,'grp'=48] {'grp'}, use_global_device_ids=true, to_apply=%region_2.0 | all-reduce | flops 4096 | bytes 32768 | tf_op jit(solution)/shard_map/psum | solution.py:18
  687.6 0.6 select_reduce_fusion.1
  688.8 0.1 copy.7
  688.9 5.8 cholesky.17
  694.8 0.6 compare_reduce_fusion
  695.5 0.7 fusion
  696.1 4.9 custom-call.6
  701.0 0.1 fusion.1
  701.2 2.9 fusion.4
  704.1 0.0 all-reduce.2.cloned.1.call-update
  704.1 472.6 %all-reduce.2.cloned.1.call-done = f32[4096,64]{0,1:T(8,128)} async-done(((f32[4096,64]{0,1:T(8,128)}), f32[4096,64]{0,1:T(8,128)}) %all-reduce.2.cloned.1.call-update) | async-done | bytes 1048592 | tf_op jit(solution)/shard_map/psum | solution.py:25
  1176.8 1.3 broadcast_multiply_fusion
  1178.1 0.0 copy-done.4
  1178.1 0.0 copy-done.3
  1178.1 0.0 copy-start.1
  1178.1 1.3 multiply_subtract_fusion
  1179.4 0.0 copy-done.1
  (3 shorter events, 0.1 us)
Async XLA Ops:
  7.2 454.4 %copy-start = (f32[4096,64]{0,1:T(8,128)S(1)}, f32[4096,64]{0,1:T(8,128)}, u32[]{:S(2)}) copy-start(f32[4096,64]{0,1:T(8,128)} %param.7) | copy-start | bytes 3145732
  7.2 454.4 %copy-start.2 = (f32[1,8,4096]{2,1,0:T(8,128)S(1)}, f32[1,8,4096]{2,1,0:T(8,128)}, u32[]{:S(2)}) copy-start(f32[1,8,4096]{2,1,0:T(8,128)} %param.5) | copy-start | bytes 393220
  7.2 454.4 %reduce-scatter.2.cloned.1.call-start = ((), (), s32[]{:S(2)}) async-start(), calls=%async_computation.1 | async-start | bytes 6422528 | tf_op jit(solution)/shard_map/reduce_scatter | solution.py:13
  12.6 1165.4 %copy-start.4 = (f32[8,4096]{1,0:T(8,128)S(1)}, f32[8,4096]{1,0:T(8,128)}, u32[]{:S(2)}) copy-start(f32[8,4096]{1,0:T(8,128)} %param.6) | copy-start | bytes 393220
  12.7 1164.1 %all-reduce.2.cloned.1.call-start = ((), (), s32[]{:S(2)}) async-start(), calls=%async_computation.2 | async-start | bytes 2097152 | tf_op jit(solution)/shard_map/psum | solution.py:25
  461.6 716.5 %copy-start.3 = (f32[8,4096]{1,0:T(8,128)S(1)}, f32[8,4096]{1,0:T(8,128)}, u32[]{:S(2)}) copy-start(f32[8,4096]{1,0:T(8,128)} %reduce-scatter.2.cloned.1.call-done) | copy-start | bytes 393220
  1178.1 1.3 copy-start.1
Sparse Core Ops, SparseCore 0:
  13.1 448.4 reduce-scatter.1
  704.2 472.4 all-reduce.1
where the time goes:
time: 1190 us
  waiting for transfers between devices  922 us (77%)
  blocking collectives  224 us (19%)
  other arithmetic  19.4 us (2%)
  between operations  14.8 us (1%)
    psum x1, waiting for transfers between devices, on_device(): q_next = lax.psum(full_dot(corrected.T, left_hat), ('rep', 'grp')) / groups  473 us
    reduce_scatter x1, waiting for transfers between devices, on_device(): summed = lax.psum_scatter(term, 'grp', scatter_dimension=0, tiled=True)  449 us
    psum x1, blocking collectives, on_device(): gram = lax.psum(full_dot(left.T, left), 'grp')  200 us
  transfers between devices with their start and end apart: 2, of which 2 were waited for; matrix products, arithmetic and copies ran while one was open for 0% of the time, Pallas kernels for 0%

commit v1 on v0

v1 whole, which is shorter than its diff:
```python
import jax
import jax.numpy as jnp
from jax import lax
from jax.sharding import Mesh, PartitionSpec as P

NY, NC, NZ, NX = 8, 2, 12, 4
REP, GRP = ("y", "core"), ("z", "x")
F32, BF16 = jnp.float32, jnp.bfloat16


def full_dot(left, right):
    return jnp.dot(left, right, precision=lax.Precision.HIGHEST)


def parts_of(value):
    high = lax.reduce_precision(value, 8, 7)
    rest = value - high
    middle = lax.reduce_precision(rest, 8, 7)
    return [p.astype(BF16) for p in (high, middle, rest - middle)]


def exchange(value, axes):
    return lax.all_to_all(value, axes, 0, 0, tiled=True)


def gathered(value, axes, n):
    return exchange(jnp.broadcast_to(value[None], (n,) + value.shape), axes)


def scatter(value, axis):
    return lax.psum_scatter(value, axis, scatter_dimension=0, tiled=True)


def on_device(grad_terms, error_buffer, weight, q_prev):
    term, error = grad_terms[0, 0], error_buffer[0]
    rows, width = term.shape
    rank = q_prev.shape[1]
    n_rep, n_grp = NY * NC, NZ * NX
    own = rows // n_grp
    at = (lax.axis_index("z") * NX + lax.axis_index("x")) * own

    half = width // 2
    first = term[:, :half].reshape(NZ, NX, own, half).transpose(1, 0, 2, 3)
    first = scatter(first.reshape(rows, half).astype(F32), "x")
    second = scatter(term[:, half:].astype(F32), "z")
    first = scatter(first, "z")
    second = scatter(second, "x")

    q_parts = jnp.concatenate(parts_of(q_prev.T), axis=0)
    left = lax.dot_general(term, q_parts, (((1,), (1,)), ((), ())), preferred_element_type=F32)
    left = left[:, :rank] + left[:, rank : 2 * rank] + left[:, 2 * rank :]
    mine = lax.dynamic_slice_in_dim(left, at, own, 0) + full_dot(error, q_prev)
    left = lax.dynamic_update_slice_in_dim(left, mine, at, 0)
    block = exchange(left.reshape(n_rep, rows // n_rep, rank), REP).sum(0)
    block = gathered(block, GRP, n_grp).sum(0)
    left = gathered(block, REP, n_rep).reshape(rows, rank)
    left_own = lax.dynamic_slice_in_dim(left, at, own, 0)

    turned = parts_of(left.T)
    right = sum(jnp.dot(p, term, preferred_element_type=F32) for p in turned)
    right = right + full_dot(left_own.T, error)
    cols = width // n_rep
    right = right.reshape(rank, n_rep, cols).transpose(1, 0, 2)
    right = exchange(right, REP).sum(0)
    lanes = 128
    flat = right.reshape(rank, cols // lanes, lanes).transpose(1, 0, 2)
    flat = flat.reshape(rank * cols // lanes, lanes)
    pieces = -(-flat.shape[0] // n_grp)
    flat = jnp.pad(flat, ((0, pieces * n_grp - flat.shape[0]), (0, 0)))
    piece = exchange(flat.reshape(n_grp, pieces, lanes), GRP).sum(0)
    flat = gathered(piece, GRP, n_grp).reshape(n_grp * pieces, lanes)
    flat = flat[: rank * cols // lanes].reshape(cols // lanes, rank, lanes)
    right = flat.transpose(1, 0, 2).reshape(rank, cols)

    gram = full_dot(left.T, left)
    shift = 0.01 * (jnp.trace(gram) / rank + 1e-06)
    eye = jnp.eye(rank, dtype=F32)
    lower = jnp.linalg.cholesky(gram + shift * eye)
    inverse = lax.linalg.triangular_solve(lower, eye, left_side=True, lower=True)

    right = full_dot(inverse, right) / n_rep
    q_turned = gathered(right, REP, n_rep).transpose(1, 0, 2).reshape(rank, width)
    left_hat = full_dot(left_own, inverse.T)
    approx = full_dot(left_hat, q_turned)
    corrected = jnp.concatenate([first, second], axis=1) + error
    return (q_turned.T, (corrected - approx)[None], weight - 0.5 * approx)


def solution(mesh):
    split = Mesh(mesh.devices.reshape(NY, NC, NZ, NX), REP + GRP)
    placed = (P(REP, GRP, None, None), P(REP, GRP, None), P(GRP, None), P())
    return jax.shard_map(
        on_device,
        mesh=split,
        in_specs=placed,
        out_specs=(P(), P(REP, GRP, None), P(GRP, None)),
        check_vma=False,
    )
```

time: 1190 us -> 270 us (0.23)
  waiting for transfers between devices: 922 us -> 111 us
  blocking collectives: 224 us -> 65 us
  starting transfers between devices: 0.08 us -> 22.9 us
  local copies, waits for them, and re-layouts: 0.1 us -> 17.3 us
    psum x1 -> x0, waiting for transfers between devices: 473 us -> none  [on_device(): q_next = lax.psum(full_dot(corrected.T, left_hat), ('rep', 'grp')) / groups]
    reduce_scatter x1 -> x4, waiting for transfers between devices: 449 us -> 48.8 us  [scatter(): return lax.psum_scatter(value, axis, scatter_dimension=0, tiled=True)]
    psum x2 -> x0, blocking collectives: 224 us -> none  [the longest x1 200 us: on_device(): gram = lax.psum(full_dot(left.T, left), 'grp')]
    all_to_all x0 -> x3, blocking collectives: none -> 65 us  [exchange(): return lax.all_to_all(value, axes, 0, 0, tiled=True)]
    all_to_all x0 -> x4, waiting for transfers between devices: none -> 61.4 us  [exchange(): return lax.all_to_all(value, axes, 0, 0, tiled=True)]
    all_to_all x0 -> x4, starting transfers between devices: none -> 22.8 us  [exchange(): return lax.all_to_all(value, axes, 0, 0, tiled=True)]
  transfers between devices with their start and end apart: 2 -> 8, of which waited for: 2 -> 5; matrix products, arithmetic and copies ran while one was open for 0% -> 18% of each run, Pallas kernels for 0% -> 0%
where the time goes in v1:
time: 270 us; the launch traced here: 269 us
  waiting for transfers between devices  111 us (41%)
  blocking collectives  65 us (24%)
  other arithmetic  27.2 us (10%)
  starting transfers between devices  22.9 us (8%)
  local copies, waits for them, and re-layouts  17.3 us (6%)
  between operations  14.7 us (5%)
  matrix products  11.2 us (4%)
    all_to_all x3, blocking collectives, exchange(): return lax.all_to_all(value, axes, 0, 0, tiled=True)  65 us
    all_to_all x4, waiting for transfers between devices, exchange(): return lax.all_to_all(value, axes, 0, 0, tiled=True)  61.4 us
    reduce_scatter x4, waiting for transfers between devices, scatter(): return lax.psum_scatter(value, axis, scatter_dimension=0, tiled=True)  48.8 us
    all_to_all x4, starting transfers between devices, exchange(): return lax.all_to_all(value, axes, 0, 0, tiled=True)  22.8 us
    unnamed x16, local copies, waits for them, and re-layouts  7.65 us
    another operation x3, other arithmetic, on_device(): lower = jnp.linalg.cholesky(gram + shift * eye)  6.52 us
    dot_general x6, matrix products, full_dot(): return jnp.dot(left, right, precision=lax.Precision.HIGHEST)  6.35 us
    all_to_all x3, other arithmetic, exchange(): return lax.all_to_all(value, axes, 0, 0, tiled=True)  6.04 us
  transfers between devices with their start and end apart: 8, of which 5 were waited for; matrix products, arithmetic and copies ran while one was open for 18% of the time, Pallas kernels for 0%

profile of v1, /device:TPU:6, one launch (start us, length us, event | category | flops | bytes accessed | tf_op | source)
XLA Modules:
  0.0 269.2 jit_solution(1529379541059531648)
XLA Ops:
  7.2 4.0 %fusion.33 = (bf16[384,2048]{1,0:T(8,128)(2,1)S(1)}, f32[384,2048]{1,0:T(8,128)}) fusion(bf16[384,4096]{1,0:T(8,128)(2,1)} %bitcast.84), kind=kLoop, calls=%fused_computation.60 | loop fusion | flops 786432 | bytes 7864320 | tf_op jit(solution)/shard_map/slice | solution.py:43
  11.3 0.4 convert_bitcast_fusion
  11.6 1.9 copy.43
  13.6 2.7 %reduce-precision_convert_fusion.1 = (bf16[64,4096]{1,0:T(8,128)(2,1)}, bf16[64,4096]{1,0:T(8,128)(2,1)}, bf16[64,4096]{1,0:T(8,128)(2,1)}) fusion(f32[4096,64]{0,1:T(8,128)} %param.7), kind=kLoop, calls=%fused_computation.14 | loop fusion | flops 1835008 | bytes 2621440 | tf_op jit(solution)/shard_map/convert_element_type | solution.py:19
  16.3 2.6 fusion.6
  18.9 0.7 slice_add_fusion
  19.6 1.7 convolution_add_fusion.3
  21.3 1.6 dynamic_update_slice.3
  22.9 1.0 copy.37
  23.9 0.8 reshape.68
  24.7 15.5 %all_to_all.35 = f32[16,1,1536]{2,1,0:T(1,128)S(1)} all-to-all(f32[16,1,1536]{2,1,0:T(1,128)} %reshape.68), channel_id=1, replica_groups=mesh['y'=8,'core'=2,'z'=12,'x'=4] {'y','core'}, dimensions={0} | all-to-all | bytes 196608 | tf_op jit(solution)/shard_map/all_to_all | solution.py:23
  40.3 0.5 broadcast.57
  40.8 1.5 reduce.6
  42.3 1.0 reshape.69
  43.3 0.9 broadcast_in_dim.16
  44.2 2.1 reshape.70
  46.3 37.6 %all_to_all.36 = f32[48,1,1536]{2,1,0:T(1,128)} all-to-all(f32[48,1,1536]{2,1,0:T(1,128)} %reshape.70), channel_id=1, replica_groups=mesh['y'=8,'core'=2,'z'=12,'x'=4] {'z','x'}, dimensions={0} | all-to-all | bytes 589824 | tf_op jit(solution)/shard_map/all_to_all | solution.py:23
  83.9 3.0 %reduce.7 = f32[48,1536]{1,0:T(8,128)} reduce(f32[48,1,1536]{2,1,0:T(1,128)} %all_to_all.36, f32[]{:T(128)} %broadcast.57), dimensions={1}, to_apply=%all_to_all.22.reduce_sub_computation | reduce | bytes 589828 | tf_op jit(solution)/shard_map/all_to_all | solution.py:23
  86.9 1.9 reshape.71
  88.8 1.1 reduce_sum.47
  90.0 0.8 reshape.72
  90.8 11.9 %all_to_all.37 = f32[16,1,1536]{2,1,0:T(1,128)S(1)} all-to-all(f32[16,1,1536]{2,1,0:T(1,128)} %reshape.72), channel_id=1, replica_groups=mesh['y'=8,'core'=2,'z'=12,'x'=4] {'y','core'}, dimensions={0} | all-to-all | bytes 196608 | tf_op jit(solution)/shard_map/all_to_all | solution.py:23
  102.7 1.5 reduce.8
  104.2 1.0 reshape.73
  105.3 0.7 fusion.30
  105.9 0.7 convolution_add_fusion.2
  106.6 0.7 convolution_add_fusion.1
  107.3 1.0 convolution_add_fusion
  108.3 1.1 copy.53
  109.4 3.7 %all-to-all-start.3 = ((f32[16,64,256]{2,1,0:T(8,128)}), f32[16,64,256]{2,1,0:T(8,128)S(1)}, u32[]{:S(2)}, u32[]{:S(2)}) async-start(f32[16,64,256]{2,1,0:T(8,128)} %bitcast.83), calls=%async_computation.3 | async-start | bytes 2097152 | tf_op jit(solution)/shard_map/all_to_all | solution.py:23
  113.1 1.1 select_reduce_fusion.1
  114.9 5.8 %cholesky.18 = f32[64,64]{1,0:T(8,128)S(1)} custom-call(f32[64,64]{1,0:T(8,128)S(1)} %fusion.21), custom_call_target="Cholesky" | custom-call | tf_op jit(solution)/shard_map/jit(cholesky)/cholesky | solution.py:78
  120.8 0.6 compare_reduce_fusion
  121.4 18.2 %all-to-all-done.3 = f32[16,64,256]{2,1,0:T(8,128)S(1)} async-done(((f32[16,64,256]{2,1,0:T(8,128)}), f32[16,64,256]{2,1,0:T(8,128)S(1)}, u32[]{:S(2)}, u32[]{:S(2)}) %all-to-all-start.3) | async-done | bytes 1048608 | tf_op jit(solution)/shard_map/all_to_all | solution.py:23
  139.8 0.7 reshape.60
  140.5 8.2 %all-to-all-start.4 = ((f32[48,3,128]{2,1,0:T(4,128)}), f32[48,3,128]{2,1,0:T(4,128)S(1)}, u32[]{:S(2)}, u32[]{:S(2)}) async-start(f32[48,3,128]{2,1,0:T(4,128)} %reshape.60), calls=%async_computation.4 | async-start | bytes 196608 | tf_op jit(solution)/shard_map/all_to_all | solution.py:23
  148.7 0.7 fusion.17
  149.4 4.9 %custom-call.6 = f32[1,64,64]{1,2,0:T(8,128)S(1)} custom-call(f32[1,64,64]{2,1,0:T(8,128)S(1)} %fusion.17), custom_call_target="InvertDiagBlocksLowerTriangular" | custom-call | tf_op jit(solution)/shard_map/triangular_solve | solution.py:79
  154.2 5.8 %all-to-all-done.4 = f32[48,3,128]{2,1,0:T(4,128)S(1)} async-done(((f32[48,3,128]{2,1,0:T(4,128)}), f32[48,3,128]{2,1,0:T(4,128)S(1)}, u32[]{:S(2)}, u32[]{:S(2)}) %all-to-all-start.4) | async-done | bytes 73760 | tf_op jit(solution)/shard_map/all_to_all | solution.py:23
  160.1 0.7 broadcast_in_dim.19
  160.8 7.3 %all-to-all-start.5 = ((f32[48,3,128]{2,1,0:T(4,128)}), f32[48,3,128]{2,1,0:T(4,128)S(1)}, u32[]{:S(2)}, u32[]{:S(2)}) async-start(f32[48,3,128]{2,1,0:T(4,128)} %broadcast_in_dim.19), calls=%async_computation.5 | async-start | bytes 196608 | tf_op jit(solution)/shard_map/all_to_all | solution.py:23
  168.3 11.5 %all-to-all-done.5 = f32[48,3,128]{2,1,0:T(4,128)S(1)} async-done(((f32[48,3,128]{2,1,0:T(4,128)}), f32[48,3,128]{2,1,0:T(4,128)S(1)}, u32[]{:S(2)}, u32[]{:S(2)}) %all-to-all-start.5) | async-done | bytes 73760 | tf_op jit(solution)/shard_map/all_to_all | solution.py:23
  180.2 1.1 broadcast_in_dim.20
  181.2 3.7 %all-to-all-start.6 = ((f32[16,64,256]{2,1,0:T(8,128)}), f32[16,64,256]{2,1,0:T(8,128)S(1)}, u32[]{:S(2)}, u32[]{:S(2)}) async-start(f32[16,64,256]{2,1,0:T(8,128)} %broadcast_in_dim.20), calls=%async_computation.6 | async-start | bytes 2097152 | tf_op jit(solution)/shard_map/all_to_all | solution.py:23
  185.0 0.5 reduce-scatter.7.cloned.1.call-update
  185.6 25.9 %all-to-all-done.6 = f32[16,64,256]{2,1,0:T(8,128)S(1)} async-done(((f32[16,64,256]{2,1,0:T(8,128)}), f32[16,64,256]{2,1,0:T(8,128)S(1)}, u32[]{:S(2)}, u32[]{:S(2)}) %all-to-all-start.6) | async-done | bytes 1048608 | tf_op jit(solution)/shard_map/all_to_all | solution.py:23
  211.7 48.8 %reduce-scatter.7.cloned.1.call-done = f32[8,2048]{1,0:T(8,128)} async-done(((f32[96,2048]{1,0:T(8,128)}), f32[8,2048]{1,0:T(8,128)}) %reduce-scatter.7.cloned.1.call-update) | async-done | bytes 65552 | tf_op jit(solution)/shard_map/reduce_scatter | solution.py:31
  260.4 2.2 multiply_subtract_fusion
  (38 shorter events, 1.4 us)
Async XLA Ops:
  7.2 172.8 %reduce-scatter.9.cloned.1.call-start = ((), (), s32[]{:S(2)}) async-start(), calls=%async_computation.13 | async-start | bytes 3407872 | tf_op jit(solution)/shard_map/reduce_scatter | solution.py:31
  11.2 173.8 %reduce-scatter.5.cloned.1.call-start = ((), (), s32[]{:S(2)}) async-start(), calls=%async_computation.11 | async-start | bytes 3932160 | tf_op jit(solution)/shard_map/reduce_scatter | solution.py:31
  13.5 2.8 %copy-start = (bf16[1,1,384,4096]{3,2,1,0:T(8,128)(2,1)S(1)}, bf16[1,1,384,4096]{3,2,1,0:T(8,128)(2,1)}, u32[]{:S(2)}) copy-start(bf16[1,1,384,4096]{3,2,1,0:T(8,128)(2,1)} %param.4) | copy-start | bytes 9437188
  16.3 3.3 %copy-start.1 = (f32[4096,64]{0,1:T(8,128)S(1)}, f32[4096,64]{0,1:T(8,128)}, u32[]{:S(2)}) copy-start(f32[4096,64]{0,1:T(8,128)} %param.7) | copy-start | bytes 3145732
  16.3 3.3 %copy-start.3 = (f32[1,8,4096]{2,1,0:T(8,128)S(1)}, f32[1,8,4096]{2,1,0:T(8,128)}, u32[]{:S(2)}) copy-start(f32[1,8,4096]{2,1,0:T(8,128)} %param.5) | copy-start | bytes 393220
  109.4 30.3 %all-to-all-start.3 = ((f32[16,64,256]{2,1,0:T(8,128)}), f32[16,64,256]{2,1,0:T(8,128)S(1)}, u32[]{:S(2)}, u32[]{:S(2)}) async-start(f32[16,64,256]{2,1,0:T(8,128)} %bitcast.83), calls=%async_computation.3 | async-start | bytes 2097152 | tf_op jit(solution)/shard_map/all_to_all | solution.py:23
  140.5 19.6 %all-to-all-start.4 = ((f32[48,3,128]{2,1,0:T(4,128)}), f32[48,3,128]{2,1,0:T(4,128)S(1)}, u32[]{:S(2)}, u32[]{:S(2)}) async-start(f32[48,3,128]{2,1,0:T(4,128)} %reshape.60), calls=%async_computation.4 | async-start | bytes 196608 | tf_op jit(solution)/shard_map/all_to_all | solution.py:23
  160.8 19.0 %all-to-all-start.5 = ((f32[48,3,128]{2,1,0:T(4,128)}), f32[48,3,128]{2,1,0:T(4,128)S(1)}, u32[]{:S(2)}, u32[]{:S(2)}) async-start(f32[48,3,128]{2,1,0:T(4,128)} %broadcast_in_dim.19), calls=%async_computation.5 | async-start | bytes 196608 | tf_op jit(solution)/shard_map/all_to_all | solution.py:23
  168.1 43.6 %reduce-scatter.11.cloned.1.call-start = ((), (), s32[]{:S(2)}) async-start(), calls=%async_computation.14 | async-start | bytes 327680 | tf_op jit(solution)/shard_map/reduce_scatter | solution.py:31
  180.0 80.5 %copy-start.4 = (f32[8,4096]{1,0:T(8,128)S(1)}, f32[8,4096]{1,0:T(8,128)}, u32[]{:S(2)}) copy-start(f32[8,4096]{1,0:T(8,128)} %param.6) | copy-start | bytes 393220
  181.2 30.3 %all-to-all-start.6 = ((f32[16,64,256]{2,1,0:T(8,128)}), f32[16,64,256]{2,1,0:T(8,128)S(1)}, u32[]{:S(2)}, u32[]{:S(2)}) async-start(f32[16,64,256]{2,1,0:T(8,128)} %broadcast_in_dim.20), calls=%async_computation.6 | async-start | bytes 2097152 | tf_op jit(solution)/shard_map/all_to_all | solution.py:23
  184.9 75.5 %reduce-scatter.7.cloned.1.call-start = ((), (), s32[]{:S(2)}) async-start(), calls=%async_computation.12 | async-start | bytes 851968 | tf_op jit(solution)/shard_map/reduce_scatter | solution.py:31
  211.6 51.0 %copy-start.2 = (f32[16,8,8,256]{3,2,0,1:T(8,128)}, f32[16,8,8,256]{3,2,0,1:T(8,128)S(1)}, u32[]{:S(2)}) copy-start(f32[16,8,8,256]{3,2,0,1:T(8,128)S(1)} %copy.46) | copy-start | bytes 3145732
Sparse Core Ops, SparseCore 0:
  11.3 79.5 reduce-scatter.8
  94.1 41.8 reduce-scatter.4
  180.1 19.0 reduce-scatter.10
  202.4 57.9 reduce-scatter.6

commit v2 on v1

v2 whole, which is shorter than its diff:
```python
import functools

import jax
import jax.numpy as jnp
from jax import lax
from jax.experimental import pallas as pl
from jax.experimental.pallas import tpu as pltpu
from jax.sharding import Mesh, PartitionSpec as P

NY, NC, NZ, NX = 8, 2, 12, 4
REP, GRP = ("y", "core"), ("z", "x")
F32, BF16 = jnp.float32, jnp.bfloat16
RANK, OWN, LANES = 64, 8, 128
HIGHEST = lax.Precision.HIGHEST
MIB = 2**20


def full_dot(left, right):
    return jnp.dot(left, right, precision=HIGHEST)


def parts_of(value):
    high = value.astype(BF16).astype(F32)
    rest = value - high
    middle = rest.astype(BF16).astype(F32)
    return [high, middle, rest - middle]


def stacked(parts):
    return jnp.concatenate(parts, axis=0).astype(BF16)


def dot_nt(left, right):
    return lax.dot_general(left, right, (((1,), (1,)), ((), ())), preferred_element_type=F32)


def exchange(value, axes):
    return lax.all_to_all(value, axes, 0, 0, tiled=True)


def gathered(value, axes, n):
    return exchange(jnp.broadcast_to(value[None], (n,) + value.shape), axes)


def scatter(value, axis):
    return lax.psum_scatter(value, axis, scatter_dimension=0, tiled=True)


def swap(value):
    return lax.ppermute(value, "core", [(i, NC - 1 - i) for i in range(NC)])


def slot_of(tile):
    n_rep = NY * NC
    return tile % n_rep, tile // n_rep * OWN


def own_place(g, n_tiles):
    low = g < n_tiles
    return low, pl.multiple_of(jnp.where(low, g, g - n_tiles) * OWN, OWN)


def prepare(g_ref, term_ref, error_ref, q_ref, wide_ref, left_ref, parts, packed):
    step = pl.program_id(0)
    rows = term_ref.shape[0]

    @pl.when(step == 0)
    def _():
        for i, part in enumerate(parts_of(q_ref[...])):
            parts[i * RANK : (i + 1) * RANK] = part.astype(BF16)

    block = term_ref[...]
    for z in range(rows // (NX * OWN)):
        band = block[z * NX * OWN : (z + 1) * NX * OWN].astype(F32)
        for x in range(NX):
            wide_ref[x, z] = band[x * OWN : (x + 1) * OWN]
    product = dot_nt(block, parts[...])
    left = product[:, :RANK] + product[:, RANK : 2 * RANK] + product[:, 2 * RANK :]

    @pl.when(step == 0)
    def _():
        packed[:, :RANK] = left

    @pl.when(step == 1)
    def _():
        packed[:, RANK:] = left
        high, middle, low = parts_of(error_ref[...])
        errors = stacked([high, middle, low, jnp.zeros_like(low)])
        cross = dot_nt(errors, parts[...])
        own = cross[2 * OWN : 3 * OWN, :RANK] + cross[:OWN, 2 * RANK :]
        own = own + cross[OWN : 2 * OWN, RANK : 2 * RANK]
        own = own + cross[OWN : 2 * OWN, :RANK] + cross[:OWN, RANK : 2 * RANK]
        own = own + cross[:OWN, :RANK]
        n_tiles = rows // OWN
        first, at = own_place(g_ref[0], n_tiles)
        none = jnp.zeros_like(own)
        pair = jnp.concatenate([jnp.where(first, own, none), jnp.where(first, none, own)], axis=1)
        packed[pl.ds(at, OWN), :] += pair
        left_ref[...] = jnp.zeros_like(left_ref)
        for tile in range(n_tiles):
            device, slot = slot_of(tile)
            left_ref[device, slot : slot + OWN] = packed[tile * OWN : (tile + 1) * OWN]


def right_terms(s_ref, left_ref, term_ref, error_ref, send_ref, keep_ref, own_ref, packed, parts):
    step = pl.program_id(0)
    half = term_ref.shape[0] // 2
    n_tiles = half // OWN
    first, at = own_place(s_ref[0], n_tiles)

    @pl.when(step == 0)
    def _():
        for tile in range(n_tiles):
            device, slot = slot_of(tile)
            packed[tile * OWN : (tile + 1) * OWN] = left_ref[device, slot : slot + OWN]
        turned = packed[...].T
        for i in range(2):
            for j, part in enumerate(parts_of(turned[i * RANK : (i + 1) * RANK])):
                parts[i, j * RANK : (j + 1) * RANK] = part.astype(BF16)
        pair = packed[pl.ds(at, OWN), :]
        own_ref[...] = jnp.where(first, pair[:, :RANK], pair[:, RANK:])

    total = jnp.dot(parts[0], term_ref[:half], preferred_element_type=F32)
    total = total + jnp.dot(parts[1], term_ref[half:], preferred_element_type=F32)
    total = total[:RANK] + total[RANK : 2 * RANK] + total[2 * RANK :]
    total = total + lax.dot_general(
        own_ref[...], error_ref[...], (((0,), (0,)), ((), ())), precision=HIGHEST, preferred_element_type=F32
    )
    count, cols = send_ref.shape[0], send_ref.shape[2]

    @pl.when(step < 2)
    def _():
        for k in range(count):
            send_ref[k] = total[:, k * cols : (k + 1) * cols]

    @pl.when(step >= 2)
    def _():
        for k in range(count):
            keep_ref[k] = total[:, k * cols : (k + 1) * cols]


def fold(blocks_ref, _, flat_ref):
    total = blocks_ref[0]
    for i in range(1, blocks_ref.shape[0]):
        total = total + blocks_ref[i]
    flat_ref[...] = jnp.zeros_like(flat_ref)
    for i in range(total.shape[1] // LANES):
        flat_ref[i * RANK : (i + 1) * RANK] = total[:, i * LANES : (i + 1) * LANES]


def finish(s_ref, mine_ref, other_ref, left_ref, summed_ref, error_ref, weight_ref, q_ref, error_out, weight_out):
    step = pl.program_id(0)
    cols = mine_ref.shape[2]

    def run(blocks_ref):
        for k in range(blocks_ref.shape[0]):
            at = slice(k * cols, (k + 1) * cols)
            block = blocks_ref[k]
            q_ref[:, at] = block
            approx = jnp.dot(left_ref[...], block, precision=HIGHEST, preferred_element_type=F32)
            error_out[:, at] = summed_ref[:, at] + error_ref[:, at] - approx
            weight_out[:, at] = weight_ref[:, at] - 0.5 * approx

    pl.when(step == s_ref[1])(functools.partial(run, mine_ref))
    pl.when(step != s_ref[1])(functools.partial(run, other_ref))


def call(kernel, room, grid, in_specs, out_specs, out_shape, scratch=()):
    return pl.pallas_call(
        kernel,
        out_shape=out_shape,
        grid_spec=pltpu.PrefetchScalarGridSpec(
            num_scalar_prefetch=1, grid=grid, in_specs=in_specs, out_specs=out_specs, scratch_shapes=list(scratch)
        ),
        compiler_params=pltpu.CompilerParams(vmem_limit_bytes=room * MIB),
    )


def whole(shape):
    return pl.BlockSpec(shape, lambda *_: (0,) * len(shape))


def on_device(grad_terms, error_buffer, weight, q_prev):
    term, error = grad_terms[0, 0], error_buffer[0]
    rows, width = term.shape
    n_rep, n_grp = NY * NC, NZ * NX
    half, cols, slots = rows // 2, width // n_rep, -(-rows // 2 // OWN // n_rep) * OWN
    array = lambda *shape: jax.ShapeDtypeStruct(shape, F32)
    core = lax.axis_index("core")
    place = jnp.stack([lax.axis_index("z") * NX + lax.axis_index("x"), core]).astype(jnp.int32)

    wide, left = call(
        prepare,
        60,
        (2,),
        [
            pl.BlockSpec((half, width), lambda i, _: (i, 0)),
            whole((OWN, width)),
            whole((RANK, width)),
        ],
        [pl.BlockSpec((NX, NZ // 2, OWN, width), lambda i, _: (0, i, 0, 0)), whole((n_rep, slots, LANES))],
        [array(NX, NZ, OWN, width), array(n_rep, slots, LANES)],
        [pltpu.VMEM((3 * RANK, width), BF16), pltpu.VMEM((half, LANES), F32)],
    )(place, term, error, q_prev.T)

    summed_x = scatter(wide.reshape(rows, width), "x")
    summed = scatter(summed_x, "z")

    block = exchange(left, REP).sum(0)
    block = gathered(block, GRP, n_grp).sum(0)
    left = gathered(block, REP, n_rep)

    send, keep, left_own = call(
        right_terms,
        24,
        (4,),
        [
            whole((n_rep, slots, LANES)),
            pl.BlockSpec((rows, width // 4), lambda i, s: (0, (i + 2 - 2 * s[1]) % 4)),
            pl.BlockSpec((OWN, width // 4), lambda i, s: (0, (i + 2 - 2 * s[1]) % 4)),
        ],
        [
            pl.BlockSpec((NY // 2, RANK, cols), lambda i, _: (jnp.minimum(i, 1), 0, 0)),
            pl.BlockSpec((NY // 2, RANK, cols), lambda i, _: (jnp.maximum(i - 2, 0), 0, 0)),
            whole((OWN, RANK)),
        ],
        [array(NY, RANK, cols), array(NY, RANK, cols), array(OWN, RANK)],
        [pltpu.VMEM((half, LANES), F32), pltpu.VMEM((2, 3 * RANK, half), BF16)],
    )(place, left, term, error)
    right = exchange(keep + swap(send), "y")
    used = RANK * cols // LANES
    pieces = -(-used // n_grp)
    flat = pl.pallas_call(
        fold,
        out_shape=array(pieces * n_grp, LANES),
        in_specs=[pl.BlockSpec(memory_space=pltpu.VMEM), pl.BlockSpec(memory_space=pl.ANY)],
        out_specs=pl.BlockSpec(memory_space=pltpu.VMEM),
        compiler_params=pltpu.CompilerParams(vmem_limit_bytes=4 * MIB),
    )(right, summed_x)
    piece = exchange(flat.reshape(n_grp, pieces, LANES), GRP).sum(0)
    flat = gathered(piece, GRP, n_grp).reshape(n_grp * pieces, LANES)
    right = flat[:used].reshape(cols // LANES, RANK, LANES).transpose(1, 0, 2).reshape(RANK, cols)

    both = left.reshape(n_rep * slots, LANES)
    both = full_dot(both.T, both)
    gram = both[:RANK, :RANK] + both[RANK:, RANK:]
    shift = 0.01 * (jnp.trace(gram) / RANK + 1e-06)
    eye = jnp.eye(RANK, dtype=F32)
    lower = jnp.linalg.cholesky(gram + shift * eye)
    inverse = lax.linalg.triangular_solve(lower, eye, left_side=True, lower=True)
    left_hat = full_dot(left_own, inverse.T)

    right = full_dot(inverse, right) / n_rep
    mine = gathered(right, "y", NY)
    other = swap(mine)
    side = pl.BlockSpec((OWN, width // 2), lambda i, _: (0, i))
    q_turned, error_next, weight_next = call(
        finish,
        16,
        (2,),
        [whole((NY, RANK, cols)), whole((NY, RANK, cols)), whole((OWN, RANK)), side, side, side],
        [pl.BlockSpec((RANK, width // 2), lambda i, _: (0, i)), side, side],
        [array(RANK, width), array(OWN, width), array(OWN, width)],
    )(place, mine, other, left_hat, summed, error, weight)
    return (q_turned.T, error_next[None], weight_next)


def solution(mesh):
    split = Mesh(mesh.devices.reshape(NY, NC, NZ, NX), REP + GRP)
    placed = (P(REP, GRP, None, None), P(REP, GRP, None), P(GRP, None), P())
    return jax.shard_map(
        on_device,
        mesh=split,
        in_specs=placed,
        out_specs=(P(), P(REP, GRP, None), P(GRP, None)),
        check_vma=False,
    )
```

time: 270 us -> 203 us (0.75); the launches traced: 269 us -> 199 us
  waiting for transfers between devices: 111 us -> 36.3 us
  blocking collectives: 65 us -> 82.2 us
  local copies, waits for them, and re-layouts: 17.3 us -> 4.12 us
  Pallas kernels: 0 us -> 12.8 us
  other arithmetic: 27.2 us -> 16.7 us
  matrix products: 11.2 us -> 0.93 us
  starting transfers between devices: 22.9 us -> 31.4 us
    reduce_scatter x4 -> x2, waiting for transfers between devices: 48.8 us -> 7.36 us  [scatter(): return lax.psum_scatter(value, axis, scatter_dimension=0, tiled=True)]
    all_to_all x4 -> x3, waiting for transfers between devices: 61.4 us -> 27.1 us  [exchange(): return lax.all_to_all(value, axes, 0, 0, tiled=True)]
    all_to_all x3 -> x4, blocking collectives: 65 us -> 82.2 us  [exchange(): return lax.all_to_all(value, axes, 0, 0, tiled=True)]
    pallas_call x0 -> x4, Pallas kernels: none -> 12.8 us  [the longest x1 6.6 us: on_device(): call(prepare, 60, (2,), [pl.BlockSpec((half, width), lambda i, _: (i, 0))...]
    dot_general x10 -> x3, matrix products: 11 us -> 0.72 us  [full_dot(): return jnp.dot(left, right, precision=HIGHEST)]
    all_to_all x3 -> x0, other arithmetic: 6.04 us -> none  [exchange(): return lax.all_to_all(value, axes, 0, 0, tiled=True)]
    unnamed x16, local copies, waits for them, and re-layouts: 7.65 us -> 2.55 us
    ppermute x0 -> x2, starting transfers between devices: none -> 4.64 us  [swap(): return lax.ppermute(value, 'core', [(i, NC - 1 - i) for i in range(NC)])]
  transfers between devices with their start and end apart: 8 -> 7, of which waited for: 5 -> 5; matrix products, arithmetic and copies ran while one was open for 18% -> 9% of each run, Pallas kernels for 0% -> 2%
where the time goes in v2:
time: 203 us; the launch traced here: 199 us
  blocking collectives  82.2 us (40%)
  waiting for transfers between devices  36.3 us (18%)
  starting transfers between devices  31.4 us (15%)
  other arithmetic  16.7 us (8%)
  between operations  14.9 us (7%)
  Pallas kernels  12.8 us (6%)
  local copies, waits for them, and re-layouts  4.12 us (2%)
    all_to_all x4, blocking collectives, exchange(): return lax.all_to_all(value, axes, 0, 0, tiled=True)  82.2 us
    all_to_all x3, waiting for transfers between devices, exchange(): return lax.all_to_all(value, axes, 0, 0, tiled=True)  27.1 us
    all_to_all x3, starting transfers between devices, exchange(): return lax.all_to_all(value, axes, 0, 0, tiled=True)  26.7 us
    reduce_scatter x2, waiting for transfers between devices, scatter(): return lax.psum_scatter(value, axis, scatter_dimension=0, tiled=True)  7.36 us
    pallas_call x1, Pallas kernels, on_device(): call(prepare, 60, (2,), [pl.BlockSpec((half, width), lambda i, _: (i, 0))...  6.6 us
    another operation x3, other arithmetic, on_device(): lower = jnp.linalg.cholesky(gram + shift * eye)  6.52 us
    another operation x2, other arithmetic, on_device(): lax.linalg.triangular_solve(lower, eye, left_side=True, lower=True)  5.55 us
    ppermute x2, starting transfers between devices, swap(): return lax.ppermute(value, 'core', [(i, NC - 1 - i) for i in range(NC)])  4.64 us
  transfers between devices with their start and end apart: 7, of which 5 were waited for; matrix products, arithmetic and copies ran while one was open for 9% of the time, Pallas kernels for 2%

profile of v2, /device:TPU:6, one launch (start us, length us, event | category | flops | bytes accessed | tf_op | source)
XLA Modules:
  0.0 199.3 jit_solution(14896668155748832965)
XLA Ops:
  7.2 0.0 reduce-scatter.3.cloned.1.call-start
  7.2 0.6 pad_add_fusion.g_ref.s_ref
  7.8 6.6 %shard_map.67 = (f32[4,12,8,4096]{3,2,1,0:T(8,128)}, f32[16,16,128]{2,1,0:T(8,128)}) custom-call(s32[2]{0:T(128)} %pad_add_fusion.g_ref.s_ref, bf16[384,4096]{1,0:T(8,128)(2,1)} %bitcast.30, f32[8,4096]{1,0:T(8,128)} %bitcast.32, f32[64,4096]{1,0:T(8,128)} %bitcast.36), custom_call_target="tpu_custom_call" | custom-call | tf_op jit(solution)/shard_map/pallas_call | solution.py:192
  14.4 0.0 copy-start.2
  14.4 0.0 copy-start.6
  14.4 0.0 reduce-scatter.3.cloned.1.call-update
  14.5 0.0 reduce-scatter.5.cloned.1.call-start
  14.5 0.8 copy-done.7
  15.3 15.9 %all_to_all.35 = f32[16,16,128]{2,1,0:T(8,128)S(1)} all-to-all(f32[16,16,128]{2,1,0:T(8,128)S(1)} %copy-done.7), channel_id=1, replica_groups=mesh['y'=8,'core'=2,'z'=12,'x'=4] {'y','core'}, dimensions={0} | all-to-all | bytes 262144 | tf_op jit(solution)/shard_map/all_to_all | solution.py:38
  31.2 36.6 %all_to_all.36 = f32[48,16,128]{2,1,0:T(8,128)} all-to-all(f32[48,16,128]{2,1,0:T(8,128)S(1)} %broadcast_in_dim.16), channel_id=1, replica_groups=mesh['y'=8,'core'=2,'z'=12,'x'=4] {'z','x'}, dimensions={0} | all-to-all | bytes 786432 | tf_op jit(solution)/shard_map/all_to_all | solution.py:38
  67.9 1.1 reduce_sum.38
  69.0 11.7 %all_to_all.37.left_ref = f32[16,16,128]{2,1,0:T(8,128)S(1)} all-to-all(f32[16,16,128]{2,1,0:T(8,128)S(1)} %broadcast_in_dim.17), channel_id=1, replica_groups=mesh['y'=8,'core'=2,'z'=12,'x'=4] {'y','core'}, dimensions={0} | all-to-all | bytes 262144 | tf_op jit(solution)/shard_map/all_to_all | solution.py:38
  80.7 0.0 copy-done.2
  80.7 4.1 %shard_map.68 = (f32[8,64,256]{2,1,0:T(8,128)}, f32[8,64,256]{2,1,0:T(8,128)S(1)}, f32[8,64]{1,0:T(8,128)S(1)}) custom-call(s32[2]{0:T(128)S(1)} %copy-done.6, f32[16,16,128]{2,1,0:T(8,128)S(1)} %all_to_all.37.left_ref, bf16[384,4096]{1,0:T(8,128)(2,1)S(1)} %bitcast.31, f32[8,4096]{1,0:T(8,128)S(1)} %bitcast.33), custom_call_target="tpu_custom_call" | custom-call | tf_op jit(solution)/shard_map/pallas_call | solution.py:213
  84.7 0.8 copy-done.3
  85.6 2.7 %collective-permute-start = (f32[8,64,256]{2,1,0:T(8,128)}, f32[8,64,256]{2,1,0:T(8,128)S(1)}, u32[]{:S(2)}, u32[]{:S(2)}) collective-permute-start(f32[8,64,256]{2,1,0:T(8,128)} %get-tuple-element.13), channel_id=1, source_target_pairs={{0,48},{48,0},{1,49},{49,1},{2,50},{50,2},{3,51},{51,3},{4,52},{52... | collective-permute-start | bytes 1572872 | tf_op jit(solution)/shard_map/ppermute | solution.py:50
  88.3 7.4 %reduce-scatter.3.cloned.1.call-done._ = f32[96,4096]{1,0:T(8,128)} async-done(((f32[384,4096]{1,0:T(8,128)}), f32[96,4096]{1,0:T(8,128)}) %reduce-scatter.3.cloned.1.call-update) | async-done | bytes 1572880 | tf_op jit(solution)/shard_map/reduce_scatter | solution.py:46
  95.7 0.0 reduce-scatter.5.cloned.1.call-update
  95.7 0.0 collective-permute-done
  95.7 2.0 %add.35 = f32[8,64,256]{2,1,0:T(8,128)} add(f32[8,64,256]{2,1,0:T(8,128)} %copy-done.3, f32[8,64,256]{2,1,0:T(8,128)S(1)} %collective-permute-done) | non-fusion elementwise | flops 131072 | bytes 1572864 | tf_op jit(solution)/shard_map/add | solution.py:230
  97.7 6.8 %all-to-all-start.3 = ((f32[8,64,256]{2,1,0:T(8,128)}), f32[8,64,256]{2,1,0:T(8,128)S(1)}, u32[]{:S(2)}, u32[]{:S(2)}) async-start(f32[8,64,256]{2,1,0:T(8,128)} %add.35), calls=%async_computation.3 | async-start | bytes 1048576 | tf_op jit(solution)/shard_map/all_to_all | solution.py:38
  104.5 0.4 convolution_bitcast_fusion
  104.9 0.7 select_reduce_fusion.1
  106.2 0.1 select_add_fusion
  106.3 0.1 copy.10
  106.4 0.1 fusion.5
  106.5 5.8 %cholesky.18 = f32[64,64]{1,0:T(8,128)S(1)} custom-call(f32[64,64]{1,0:T(8,128)S(1)} %fusion.5), custom_call_target="Cholesky" | custom-call | tf_op jit(solution)/shard_map/jit(cholesky)/cholesky | solution.py:249
  112.4 0.6 compare_reduce_fusion
  113.0 9.1 %all-to-all-done.3.blocks_ref = f32[8,64,256]{2,1,0:T(8,128)S(1)} async-done(((f32[8,64,256]{2,1,0:T(8,128)}), f32[8,64,256]{2,1,0:T(8,128)S(1)}, u32[]{:S(2)}, u32[]{:S(2)}) %all-to-all-start.3) | async-done | bytes 524320 | tf_op jit(solution)/shard_map/all_to_all | solution.py:38
  122.1 0.7 reshape.36
  122.8 13.8 %all-to-all-start.4 = ((f32[48,3,128]{2,1,0:T(4,128)}), f32[48,3,128]{2,1,0:T(4,128)S(1)}, u32[]{:S(2)}, u32[]{:S(2)}) async-start(f32[48,3,128]{2,1,0:T(4,128)} %reshape.36), calls=%async_computation.5 | async-start | bytes 196608 | tf_op jit(solution)/shard_map/all_to_all | solution.py:38
  136.5 0.7 fusion.2
  137.2 4.9 %custom-call.6 = f32[1,64,64]{1,2,0:T(8,128)S(1)} custom-call(f32[1,64,64]{2,1,0:T(8,128)S(1)} %fusion.2), custom_call_target="InvertDiagBlocksLowerTriangular" | custom-call | tf_op jit(solution)/shard_map/triangular_solve | solution.py:250
  142.1 7.1 %all-to-all-done.4 = f32[48,3,128]{2,1,0:T(4,128)S(1)} async-done(((f32[48,3,128]{2,1,0:T(4,128)}), f32[48,3,128]{2,1,0:T(4,128)S(1)}, u32[]{:S(2)}, u32[]{:S(2)}) %all-to-all-start.4) | async-done | bytes 73760 | tf_op jit(solution)/shard_map/all_to_all | solution.py:38
  149.2 0.1 reduce_sum.40
  149.2 0.7 broadcast_in_dim.19
  149.9 6.2 %all-to-all-start.5 = ((f32[48,3,128]{2,1,0:T(4,128)}), f32[48,3,128]{2,1,0:T(4,128)S(1)}, u32[]{:S(2)}, u32[]{:S(2)}) async-start(f32[48,3,128]{2,1,0:T(4,128)} %broadcast_in_dim.19), calls=%async_computation.6 | async-start | bytes 196608 | tf_op jit(solution)/shard_map/all_to_all | solution.py:38
  156.0 0.2 fusion.3
  156.3 11.0 %all-to-all-done.5 = f32[48,3,128]{2,1,0:T(4,128)S(1)} async-done(((f32[48,3,128]{2,1,0:T(4,128)}), f32[48,3,128]{2,1,0:T(4,128)S(1)}, u32[]{:S(2)}, u32[]{:S(2)}) %all-to-all-start.5) | async-done | bytes 73760 | tf_op jit(solution)/shard_map/all_to_all | solution.py:38
  167.3 0.1 copy.11
  167.4 0.2 convolution_multiply_fusion
  167.6 18.0 %all_to_all.38.mine_ref = f32[8,64,256]{2,1,0:T(8,128)S(1)} all-to-all(f32[8,64,256]{2,1,0:T(8,128)S(1)} %broadcast_in_dim.20), channel_id=1, replica_groups=mesh['y'=8,'core'=2,'z'=12,'x'=4] {'y'}, dimensions={0} | all-to-all | bytes 1048576 | tf_op jit(solution)/shard_map/all_to_all | solution.py:38
  185.6 1.9 collective-permute-start.1
  187.6 0.1 fusion.6.left_ref
  187.7 1.7 collective-permute-done.1.other_ref
  189.4 0.0 copy-done.4
  189.4 0.9 copy-done.5
  190.3 2.1 %shard_map.70 = (f32[64,4096]{1,0:T(8,128)}, f32[8,4096]{1,0:T(8,128)}, f32[8,4096]{1,0:T(8,128)}) custom-call(s32[2]{0:T(128)S(1)} %copy-done.6, f32[8,64,256]{2,1,0:T(8,128)S(1)} %all_to_all.38.mine_ref, f32[8,64,256]{2,1,0:T(8,128)S(1)} %collective-permute-done.1.other_ref, f32[8,64]{1,0:T(8,128)S(1)} %fusion.6.left_ref, f32[8,4096]{1,0:T(8,128)S(1)} %copy-done.5, ...), custom_call_target="tpu_custom_call" | custom-call | tf_op jit(solution)/shard_map/pallas_call | solution.py:257
  (18 shorter events, 0.2 us)
Async XLA Ops:
  7.2 88.5 %reduce-scatter.3.cloned.1.call-start = ((), (), s32[]{:S(2)}) async-start(), calls=%async_computation.9 | async-start | bytes 7864320 | tf_op jit(solution)/shard_map/reduce_scatter | solution.py:46
  14.4 0.9 copy-start.7
  14.4 66.3 %copy-start = (bf16[1,1,384,4096]{3,2,1,0:T(8,128)(2,1)S(1)}, bf16[1,1,384,4096]{3,2,1,0:T(8,128)(2,1)}, u32[]{:S(2)}) copy-start(bf16[1,1,384,4096]{3,2,1,0:T(8,128)(2,1)} %param.4) | copy-start | bytes 9437188
  14.4 66.3 %copy-start.2 = (f32[1,8,4096]{2,1,0:T(8,128)S(1)}, f32[1,8,4096]{2,1,0:T(8,128)}, u32[]{:S(2)}) copy-start(f32[1,8,4096]{2,1,0:T(8,128)} %param.5) | copy-start | bytes 393220
  14.4 66.3 %copy-start.6 = (s32[2]{0:T(128)S(1)}, s32[2]{0:T(128)}, u32[]{:S(2)}) copy-start(s32[2]{0:T(128)} %pad_add_fusion.g_ref.s_ref) | copy-start | bytes 28
  14.5 175.0 %reduce-scatter.5.cloned.1.call-start = ((), (), s32[]{:S(2)}) async-start(), calls=%async_computation.10 | async-start | bytes 1703936 | tf_op jit(solution)/shard_map/reduce_scatter | solution.py:46
  84.7 0.8 copy-start.3
  85.6 10.1 %collective-permute-start = (f32[8,64,256]{2,1,0:T(8,128)}, f32[8,64,256]{2,1,0:T(8,128)S(1)}, u32[]{:S(2)}, u32[]{:S(2)}) collective-permute-start(f32[8,64,256]{2,1,0:T(8,128)} %get-tuple-element.13), channel_id=1, source_target_pairs={{0,48},{48,0},{1,49},{49,1},{2,50},{50,2},{3,51},{51,3},{4,52},{52... | collective-permute-start | bytes 1572872 | tf_op jit(solution)/shard_map/ppermute | solution.py:50
  95.7 26.4 %copy-start.1 = (f32[96,4096]{1,0:T(8,128)S(1)}, f32[96,4096]{1,0:T(8,128)}, u32[]{:S(2)}) copy-start(f32[96,4096]{1,0:T(8,128)} %reduce-scatter.3.cloned.1.call-done._) | copy-start | bytes 4718596
  97.7 24.3 %all-to-all-start.3 = ((f32[8,64,256]{2,1,0:T(8,128)}), f32[8,64,256]{2,1,0:T(8,128)S(1)}, u32[]{:S(2)}, u32[]{:S(2)}) async-start(f32[8,64,256]{2,1,0:T(8,128)} %add.35), calls=%async_computation.3 | async-start | bytes 1048576 | tf_op jit(solution)/shard_map/all_to_all | solution.py:38
  104.5 84.9 %copy-start.4 = (f32[8,4096]{1,0:T(8,128)S(1)}, f32[8,4096]{1,0:T(8,128)}, u32[]{:S(2)}) copy-start(f32[8,4096]{1,0:T(8,128)} %weight_ref.1) | copy-start | bytes 393220
  122.8 26.4 %all-to-all-start.4 = ((f32[48,3,128]{2,1,0:T(4,128)}), f32[48,3,128]{2,1,0:T(4,128)S(1)}, u32[]{:S(2)}, u32[]{:S(2)}) async-start(f32[48,3,128]{2,1,0:T(4,128)} %reshape.36), calls=%async_computation.5 | async-start | bytes 196608 | tf_op jit(solution)/shard_map/all_to_all | solution.py:38
  149.9 17.4 %all-to-all-start.5 = ((f32[48,3,128]{2,1,0:T(4,128)}), f32[48,3,128]{2,1,0:T(4,128)S(1)}, u32[]{:S(2)}, u32[]{:S(2)}) async-start(f32[48,3,128]{2,1,0:T(4,128)} %broadcast_in_dim.19), calls=%async_computation.6 | async-start | bytes 196608 | tf_op jit(solution)/shard_map/all_to_all | solution.py:38
  185.6 3.8 %collective-permute-start.1 = (f32[8,64,256]{2,1,0:T(8,128)S(1)}, f32[8,64,256]{2,1,0:T(8,128)S(1)}, u32[]{:S(2)}, u32[]{:S(2)}) collective-permute-start(f32[8,64,256]{2,1,0:T(8,128)S(1)} %all_to_all.38.mine_ref), channel_id=1, source_target_pairs={{0,48},{48,0},{1,49},{49,1},{2,50},{50,2},{3,51},{51,3},{4,52},{52... | collective-permute-start | bytes 1572872 | tf_op jit(solution)/shard_map/ppermute | solution.py:50
  189.4 0.9 copy-start.5
Sparse Core Ops, SparseCore 0:
  14.6 81.0 reduce-scatter.2
  98.8 63.8 reduce-scatter.4

commit v3 on v2

--- a/solution.py
+++ b/solution.py
@@ -50,17 +50,12 @@
     return lax.ppermute(value, "core", [(i, NC - 1 - i) for i in range(NC)])
 
 
-def slot_of(tile):
-    n_rep = NY * NC
-    return tile % n_rep, tile // n_rep * OWN
-
-
 def own_place(g, n_tiles):
     low = g < n_tiles
     return low, pl.multiple_of(jnp.where(low, g, g - n_tiles) * OWN, OWN)
 
 
-def prepare(g_ref, term_ref, error_ref, q_ref, wide_ref, left_ref, parts, packed):
+def prepare(g_ref, term_ref, error_ref, q_ref, wide_ref, left_ref, parts):
     step = pl.program_id(0)
     rows = term_ref.shape[0]
 
@@ -79,11 +74,11 @@
 
     @pl.when(step == 0)
     def _():
-        packed[:, :RANK] = left
+        left_ref[:, :RANK] = left
 
     @pl.when(step == 1)
     def _():
-        packed[:, RANK:] = left
+        left_ref[:, RANK:] = left
         high, middle, low = parts_of(error_ref[...])
         errors = stacked([high, middle, low, jnp.zeros_like(low)])
         cross = dot_nt(errors, parts[...])
@@ -91,33 +86,24 @@
         own = own + cross[OWN : 2 * OWN, RANK : 2 * RANK]
         own = own + cross[OWN : 2 * OWN, :RANK] + cross[:OWN, RANK : 2 * RANK]
         own = own + cross[:OWN, :RANK]
-        n_tiles = rows // OWN
-        first, at = own_place(g_ref[0], n_tiles)
+        first, at = own_place(g_ref[0], rows // OWN)
         none = jnp.zeros_like(own)
         pair = jnp.concatenate([jnp.where(first, own, none), jnp.where(first, none, own)], axis=1)
-        packed[pl.ds(at, OWN), :] += pair
-        left_ref[...] = jnp.zeros_like(left_ref)
-        for tile in range(n_tiles):
-            device, slot = slot_of(tile)
-            left_ref[device, slot : slot + OWN] = packed[tile * OWN : (tile + 1) * OWN]
-
-
-def right_terms(s_ref, left_ref, term_ref, error_ref, send_ref, keep_ref, own_ref, packed, parts):
+        left_ref[pl.ds(at, OWN), :] += pair
+
+
+def right_terms(s_ref, left_ref, term_ref, error_ref, send_ref, keep_ref, own_ref, parts):
     step = pl.program_id(0)
     half = term_ref.shape[0] // 2
-    n_tiles = half // OWN
-    first, at = own_place(s_ref[0], n_tiles)
+    first, at = own_place(s_ref[0], half // OWN)
 
     @pl.when(step == 0)
     def _():
-        for tile in range(n_tiles):
-            device, slot = slot_of(tile)
-            packed[tile * OWN : (tile + 1) * OWN] = left_ref[device, slot : slot + OWN]
-        turned = packed[...].T
+        turned = left_ref[...].T
         for i in range(2):
             for j, part in enumerate(parts_of(turned[i * RANK : (i + 1) * RANK])):
                 parts[i, j * RANK : (j + 1) * RANK] = part.astype(BF16)
-        pair = packed[pl.ds(at, OWN), :]
+        pair = left_ref[pl.ds(at, OWN), :]
         own_ref[...] = jnp.where(first, pair[:, :RANK], pair[:, RANK:])
 
     total = jnp.dot(parts[0], term_ref[:half], preferred_element_type=F32)
@@ -139,23 +125,21 @@
             keep_ref[k] = total[:, k * cols : (k + 1) * cols]
 
 
-def fold(blocks_ref, _, flat_ref):
+def fold(blocks_ref, _, total_ref, __):
     total = blocks_ref[0]
     for i in range(1, blocks_ref.shape[0]):
         total = total + blocks_ref[i]
-    flat_ref[...] = jnp.zeros_like(flat_ref)
-    for i in range(total.shape[1] // LANES):
-        flat_ref[i * RANK : (i + 1) * RANK] = total[:, i * LANES : (i + 1) * LANES]
-
-
-def finish(s_ref, mine_ref, other_ref, left_ref, summed_ref, error_ref, weight_ref, q_ref, error_out, weight_out):
+    total_ref[...] = total
+
+
+def finish(s_ref, mine_ref, other_ref, inverse_ref, left_ref, summed_ref, error_ref, weight_ref, q_ref, error_out, weight_out):
     step = pl.program_id(0)
     cols = mine_ref.shape[2]
 
     def run(blocks_ref):
         for k in range(blocks_ref.shape[0]):
             at = slice(k * cols, (k + 1) * cols)
-            block = blocks_ref[k]
+            block = jnp.dot(inverse_ref[...], blocks_ref[k], precision=HIGHEST, preferred_element_type=F32)
             q_ref[:, at] = block
             approx = jnp.dot(left_ref[...], block, precision=HIGHEST, preferred_element_type=F32)
             error_out[:, at] = summed_ref[:, at] + error_ref[:, at] - approx
@@ -183,8 +167,7 @@
 def on_device(grad_terms, error_buffer, weight, q_prev):
     term, error = grad_terms[0, 0], error_buffer[0]
     rows, width = term.shape
-    n_rep, n_grp = NY * NC, NZ * NX
-    half, cols, slots = rows // 2, width // n_rep, -(-rows // 2 // OWN // n_rep) * OWN
+    half, cols = rows // 2, width // (NY * NC)
     array = lambda *shape: jax.ShapeDtypeStruct(shape, F32)
     core = lax.axis_index("core")
     place = jnp.stack([lax.axis_index("z") * NX + lax.axis_index("x"), core]).astype(jnp.int32)
@@ -198,24 +181,21 @@
             whole((OWN, width)),
             whole((RANK, width)),
         ],
-        [pl.BlockSpec((NX, NZ // 2, OWN, width), lambda i, _: (0, i, 0, 0)), whole((n_rep, slots, LANES))],
-        [array(NX, NZ, OWN, width), array(n_rep, slots, LANES)],
-        [pltpu.VMEM((3 * RANK, width), BF16), pltpu.VMEM((half, LANES), F32)],
+        [pl.BlockSpec((NX, NZ // 2, OWN, width), lambda i, _: (0, i, 0, 0)), whole((half, LANES))],
+        [array(NX, NZ, OWN, width), array(half, LANES)],
+        [pltpu.VMEM((3 * RANK, width), BF16)],
     )(place, term, error, q_prev.T)
 
-    summed_x = scatter(wide.reshape(rows, width), "x")
-    summed = scatter(summed_x, "z")
-
-    block = exchange(left, REP).sum(0)
-    block = gathered(block, GRP, n_grp).sum(0)
-    left = gathered(block, REP, n_rep)
+    tile = exchange(left.reshape(NZ * NC, half // (NZ * NC), LANES), ("z", "core")).sum(0)
+    tile = gathered(tile, ("y", "x"), NY * NX).sum(0)
+    left = gathered(tile, ("z", "core"), NZ * NC).reshape(half, LANES)
 
     send, keep, left_own = call(
         right_terms,
         24,
         (4,),
         [
-            whole((n_rep, slots, LANES)),
+            whole((half, LANES)),
             pl.BlockSpec((rows, width // 4), lambda i, s: (0, (i + 2 - 2 * s[1]) % 4)),
             pl.BlockSpec((OWN, width // 4), lambda i, s: (0, (i + 2 - 2 * s[1]) % 4)),
         ],
@@ -225,24 +205,27 @@
             whole((OWN, RANK)),
         ],
         [array(NY, RANK, cols), array(NY, RANK, cols), array(OWN, RANK)],
-        [pltpu.VMEM((half, LANES), F32), pltpu.VMEM((2, 3 * RANK, half), BF16)],
+        [pltpu.VMEM((2, 3 * RANK, half), BF16)],
     )(place, left, term, error)
-    right = exchange(keep + swap(send), "y")
-    used = RANK * cols // LANES
-    pieces = -(-used // n_grp)
-    flat = pl.pallas_call(
+    blocks = exchange((keep + swap(send)).reshape(NY * NX, RANK // NX, cols), ("y", "x"))
+
+    summed = scatter(wide.reshape(rows, width), "x")
+    vmem, anywhere = pl.BlockSpec(memory_space=pltpu.VMEM), pl.BlockSpec(memory_space=pl.ANY)
+    block, summed = pl.pallas_call(
         fold,
-        out_shape=array(pieces * n_grp, LANES),
-        in_specs=[pl.BlockSpec(memory_space=pltpu.VMEM), pl.BlockSpec(memory_space=pl.ANY)],
-        out_specs=pl.BlockSpec(memory_space=pltpu.VMEM),
-        compiler_params=pltpu.CompilerParams(vmem_limit_bytes=4 * MIB),
-    )(right, summed_x)
-    piece = exchange(flat.reshape(n_grp, pieces, LANES), GRP).sum(0)
-    flat = gathered(piece, GRP, n_grp).reshape(n_grp * pieces, LANES)
-    right = flat[:used].reshape(cols // LANES, RANK, LANES).transpose(1, 0, 2).reshape(RANK, cols)
-
-    both = left.reshape(n_rep * slots, LANES)
-    both = full_dot(both.T, both)
+        out_shape=(array(RANK // NX, cols), array(*summed.shape)),
+        in_specs=[vmem, anywhere],
+        out_specs=(vmem, anywhere),
+        input_output_aliases={1: 1},
+        compiler_params=pltpu.CompilerParams(vmem_limit_bytes=60 * MIB),
+    )(blocks, summed)
+    summed = scatter(summed, "z")
+
+    block = gathered(block, "z", NZ).sum(0)
+    mine = gathered(block, ("y", "x"), NY * NX).reshape(NY, RANK, cols)
+    other = swap(mine)
+
+    both = full_dot(left.T, left)
     gram = both[:RANK, :RANK] + both[RANK:, RANK:]
     shift = 0.01 * (jnp.trace(gram) / RANK + 1e-06)
     eye = jnp.eye(RANK, dtype=F32)
@@ -250,18 +233,15 @@
     inverse = lax.linalg.triangular_solve(lower, eye, left_side=True, lower=True)
     left_hat = full_dot(left_own, inverse.T)
 
-    right = full_dot(inverse, right) / n_rep
-    mine = gathered(right, "y", NY)
-    other = swap(mine)
     side = pl.BlockSpec((OWN, width // 2), lambda i, _: (0, i))
     q_turned, error_next, weight_next = call(
         finish,
         16,
         (2,),
-        [whole((NY, RANK, cols)), whole((NY, RANK, cols)), whole((OWN, RANK)), side, side, side],
+        [whole((NY, RANK, cols)), whole((NY, RANK, cols)), whole((RANK, RANK)), whole((OWN, RANK)), side, side, side],
         [pl.BlockSpec((RANK, width // 2), lambda i, _: (0, i)), side, side],
         [array(RANK, width), array(OWN, width), array(OWN, width)],
-    )(place, mine, other, left_hat, summed, error, weight)
+    )(place, mine, other, inverse / (NY * NC), left_hat, summed, error, weight)
     return (q_turned.T, error_next[None], weight_next)
 
 

time: 203 us -> 178 us (0.88); the launches traced: 199 us -> 177 us
  waiting for transfers between devices: 36.3 us -> 12.8 us
  blocking collectives: 82.2 us -> 99.8 us
  starting transfers between devices: 31.4 us -> 14.3 us
  Pallas kernels: 12.8 us -> 17.5 us
  other arithmetic: 16.7 us -> 13.7 us
    all_to_all x3 -> x1, waiting for transfers between devices: 27.1 us -> 6.28 us  [exchange(): return lax.all_to_all(value, axes, 0, 0, tiled=True)]
    all_to_all x4 -> x5, blocking collectives: 82.2 us -> 99.8 us  [exchange(): return lax.all_to_all(value, axes, 0, 0, tiled=True)]
    all_to_all x3 -> x1, starting transfers between devices: 26.7 us -> 10.4 us  [exchange(): return lax.all_to_all(value, axes, 0, 0, tiled=True)]
    pallas_call x1, Pallas kernels: 2.14 us -> 5.91 us  [on_device(): call(finish, 16, (2,), [whole((NY, RANK, cols)), whole((NY, RANK, cols)),...]
    reduce_scatter x2, waiting for transfers between devices: 7.36 us -> 4.63 us  [scatter(): return lax.psum_scatter(value, axis, scatter_dimension=0, tiled=True)]
  transfers between devices with their start and end apart: 7 -> 5, of which waited for: 5 -> 3; matrix products, arithmetic and copies ran while one was open for 9% -> 9% of each run, Pallas kernels for 2% -> 2%
where the time goes in v3:
time: 178 us; the launch traced here: 177 us
  blocking collectives  99.8 us (56%)
  Pallas kernels  17.5 us (10%)
  between operations  14.8 us (8%)
  starting transfers between devices  14.3 us (8%)
  other arithmetic  13.7 us (8%)
  waiting for transfers between devices  12.8 us (7%)
  local copies, waits for them, and re-layouts  3.44 us (2%)
    all_to_all x5, blocking collectives, exchange(): return lax.all_to_all(value, axes, 0, 0, tiled=True)  99.8 us
    all_to_all x1, starting transfers between devices, exchange(): return lax.all_to_all(value, axes, 0, 0, tiled=True)  10.4 us
    pallas_call x1, Pallas kernels, on_device(): call(prepare, 60, (2,), [pl.BlockSpec((half, width), lambda i, _: (i, 0))...  6.59 us
    another operation x3, other arithmetic, on_device(): lower = jnp.linalg.cholesky(gram + shift * eye)  6.52 us
    all_to_all x1, waiting for transfers between devices, exchange(): return lax.all_to_all(value, axes, 0, 0, tiled=True)  6.28 us
    pallas_call x1, Pallas kernels, on_device(): call(finish, 16, (2,), [whole((NY, RANK, cols)), whole((NY, RANK, cols)),...  5.91 us
    another operation x2, other arithmetic, on_device(): lax.linalg.triangular_solve(lower, eye, left_side=True, lower=True)  5.55 us
    reduce_scatter x2, waiting for transfers between devices, scatter(): return lax.psum_scatter(value, axis, scatter_dimension=0, tiled=True)  4.63 us
  transfers between devices with their start and end apart: 5, of which 3 were waited for; matrix products, arithmetic and copies ran while one was open for 9% of the time, Pallas kernels for 2%

profile of v3, /device:TPU:6, one launch (start us, length us, event | category | flops | bytes accessed | tf_op | source)
XLA Modules:
  0.0 177.1 jit_solution(481903010487902769)
XLA Ops:
  7.2 0.0 reduce-scatter.3.cloned.1.call-start
  7.2 0.6 pad_add_fusion.g_ref.s_ref
  7.8 6.6 %shard_map.67 = (f32[4,12,8,4096]{3,2,1,0:T(8,128)}, f32[192,128]{1,0:T(8,128)}) custom-call(s32[2]{0:T(128)} %pad_add_fusion.g_ref.s_ref, bf16[384,4096]{1,0:T(8,128)(2,1)} %bitcast.29, f32[8,4096]{1,0:T(8,128)} %bitcast.33, f32[64,4096]{1,0:T(8,128)} %bitcast.39), custom_call_target="tpu_custom_call" | custom-call | tf_op jit(solution)/shard_map/pallas_call | solution.py:175
  14.4 0.0 copy-start.5
  14.4 0.0 copy-start
  14.4 0.0 copy-start.1
  14.4 0.0 copy-start.4
  14.4 0.0 reduce-scatter.3.cloned.1.call-update
  14.4 0.0 reduce-scatter.5.cloned.1.call-start
  14.5 0.8 copy-done.5
  15.3 26.8 %all_to_all.30 = f32[24,8,128]{2,1,0:T(8,128)S(1)} all-to-all(f32[24,8,128]{2,1,0:T(8,128)S(1)} %bitcast.40), channel_id=1, replica_groups=mesh['y'=8,'core'=2,'z'=12,'x'=4] {'z','core'}, dimensions={0} | all-to-all | bytes 196608 | tf_op jit(solution)/shard_map/all_to_all | solution.py:38
  42.2 19.0 %all_to_all.31 = f32[32,8,128]{2,1,0:T(8,128)S(1)} all-to-all(f32[32,8,128]{2,1,0:T(8,128)S(1)} %broadcast_in_dim.14), channel_id=1, replica_groups=mesh['y'=8,'core'=2,'z'=12,'x'=4] {'y','x'}, dimensions={0} | all-to-all | bytes 262144 | tf_op jit(solution)/shard_map/all_to_all | solution.py:38
  61.2 14.8 %all_to_all.32 = f32[24,8,128]{2,1,0:T(8,128)S(1)} all-to-all(f32[24,8,128]{2,1,0:T(8,128)S(1)} %broadcast_in_dim.15), channel_id=1, replica_groups=mesh['y'=8,'core'=2,'z'=12,'x'=4] {'z','core'}, dimensions={0} | all-to-all | bytes 196608 | tf_op jit(solution)/shard_map/all_to_all | solution.py:38
  76.0 0.0 copy-done
  76.0 0.0 copy-done.1
  76.0 0.0 copy-done.4
  76.0 3.3 %shard_map.68 = (f32[8,64,256]{2,1,0:T(8,128)S(1)}, f32[8,64,256]{2,1,0:T(8,128)S(1)}, f32[8,64]{1,0:T(8,128)S(1)}) custom-call(s32[2]{0:T(128)S(1)} %copy-done.4, f32[192,128]{1,0:T(8,128)S(1)} %bitcast.36, bf16[384,4096]{1,0:T(8,128)(2,1)S(1)} %bitcast.30, f32[8,4096]{1,0:T(8,128)S(1)} %bitcast.34), custom_call_target="tpu_custom_call" | custom-call | tf_op jit(solution)/shard_map/pallas_call | solution.py:193
  79.3 1.9 %collective-permute-start = (f32[8,64,256]{2,1,0:T(8,128)S(1)}, f32[8,64,256]{2,1,0:T(8,128)S(1)}, u32[]{:S(2)}, u32[]{:S(2)}) collective-permute-start(f32[8,64,256]{2,1,0:T(8,128)S(1)} %get-tuple-element.15), channel_id=1, source_target_pairs={{0,48},{48,0},{1,49},{49,1},{2,50},{50,2},{3,51},{51,3},{4,52},{52... | collective-permute-start | bytes 1572872 | tf_op jit(solution)/shard_map/ppermute | solution.py:50
  81.3 1.9 %collective-permute-done = f32[8,64,256]{2,1,0:T(8,128)S(1)} collective-permute-done((f32[8,64,256]{2,1,0:T(8,128)S(1)}, f32[8,64,256]{2,1,0:T(8,128)S(1)}, u32[]{:S(2)}, u32[]{:S(2)}) %collective-permute-start) | collective-permute-done | bytes 524320 | tf_op jit(solution)/shard_map/ppermute | solution.py:50
  83.1 0.1 add.31
  83.2 22.7 %all_to_all.33.blocks_ref = f32[32,16,256]{2,1,0:T(8,128)} all-to-all(f32[32,16,256]{2,1,0:T(8,128)S(1)} %bitcast.38), channel_id=1, replica_groups=mesh['y'=8,'core'=2,'z'=12,'x'=4] {'y','x'}, dimensions={0} | all-to-all | bytes 1048576 | tf_op jit(solution)/shard_map/all_to_all | solution.py:38
  105.9 0.0 reduce-scatter.3.cloned.1.call-done._
  105.9 1.7 shard_map.69
  107.6 0.0 copy-start.2
  107.6 0.0 reduce-scatter.5.cloned.1.call-update
  107.7 0.8 broadcast_in_dim.16
  108.4 16.4 %all_to_all.34 = f32[12,16,256]{2,1,0:T(8,128)S(1)} all-to-all(f32[12,16,256]{2,1,0:T(8,128)S(1)} %broadcast_in_dim.16), channel_id=1, replica_groups=mesh['y'=8,'core'=2,'z'=12,'x'=4] {'z'}, dimensions={0} | all-to-all | bytes 393216 | tf_op jit(solution)/shard_map/all_to_all | solution.py:38
  124.9 0.9 broadcast_in_dim.18
  125.7 10.4 %all-to-all-start.5 = ((f32[32,16,256]{2,1,0:T(8,128)}), f32[32,16,256]{2,1,0:T(8,128)S(1)}, u32[]{:S(2)}, u32[]{:S(2)}) async-start(f32[32,16,256]{2,1,0:T(8,128)} %broadcast_in_dim.18), calls=%async_computation.6 | async-start | bytes 1048576 | tf_op jit(solution)/shard_map/all_to_all | solution.py:38
  136.1 0.4 convolution_bitcast_fusion
  136.5 0.7 select_reduce_fusion.1
  137.9 0.1 select_add_fusion
  138.0 0.1 copy.13
  138.0 0.1 fusion.3
  138.1 5.8 %cholesky.18 = f32[64,64]{1,0:T(8,128)S(1)} custom-call(f32[64,64]{1,0:T(8,128)S(1)} %fusion.3), custom_call_target="Cholesky" | custom-call | tf_op jit(solution)/shard_map/jit(cholesky)/cholesky | solution.py:232
  144.0 0.6 compare_reduce_fusion
  144.7 6.3 %all-to-all-done.5 = f32[32,16,256]{2,1,0:T(8,128)S(1)} async-done(((f32[32,16,256]{2,1,0:T(8,128)}), f32[32,16,256]{2,1,0:T(8,128)S(1)}, u32[]{:S(2)}, u32[]{:S(2)}) %all-to-all-start.5) | async-done | bytes 524320 | tf_op jit(solution)/shard_map/all_to_all | solution.py:38
  150.9 1.9 %collective-permute-start.1 = (f32[8,64,256]{2,1,0:T(8,128)S(1)}, f32[8,64,256]{2,1,0:T(8,128)S(1)}, u32[]{:S(2)}, u32[]{:S(2)}) collective-permute-start(f32[8,64,256]{2,1,0:T(8,128)S(1)} %bitcast.31), channel_id=1, source_target_pairs={{0,48},{48,0},{1,49},{49,1},{2,50},{50,2},{3,51},{51,3},{4,52},{52... | collective-permute-start | bytes 1572872 | tf_op jit(solution)/shard_map/ppermute | solution.py:50
  152.8 0.7 fusion
  153.5 4.9 %custom-call.6 = f32[1,64,64]{1,2,0:T(8,128)S(1)} custom-call(f32[1,64,64]{2,1,0:T(8,128)S(1)} %fusion), custom_call_target="InvertDiagBlocksLowerTriangular" | custom-call | tf_op jit(solution)/shard_map/triangular_solve | solution.py:233
  158.4 0.2 broadcast_multiply_fusion
  158.6 0.1 fusion.4.left_ref
  158.8 0.0 collective-permute-done.1.other_ref
  158.8 4.6 %reduce-scatter.5.cloned.1.call-done.summed_ref = f32[8,4096]{1,0:T(8,128)} async-done(((f32[96,4096]{1,0:T(8,128)}), f32[8,4096]{1,0:T(8,128)}) %reduce-scatter.5.cloned.1.call-update) | async-done | bytes 131088 | tf_op jit(solution)/shard_map/reduce_scatter | solution.py:46
  163.4 0.0 copy-done.2
  163.4 0.0 copy-start.3
  163.4 0.9 copy-done.3
  164.3 5.9 %shard_map.70 = (f32[64,4096]{1,0:T(8,128)}, f32[8,4096]{1,0:T(8,128)}, f32[8,4096]{1,0:T(8,128)}) custom-call(s32[2]{0:T(128)S(1)} %copy-done.4, f32[8,64,256]{2,1,0:T(8,128)S(1)} %bitcast.32, f32[8,64,256]{2,1,0:T(8,128)S(1)} %collective-permute-done.1.other_ref, f32[64,64]{1,0:T(8,128)S(1)} %get-tuple-element.23.inverse_ref, f32[8,64]{1,0:T(8,128)S(1)} %fusion.4.left_ref, ...), custom_call_target="tpu_custom_call" | custom-call | tf_op jit(solution)/shard_map/pallas_call | solution.py:237
  (6 shorter events, 0.1 us)
Async XLA Ops:
  7.2 98.8 %reduce-scatter.3.cloned.1.call-start = ((), (), s32[]{:S(2)}) async-start(), calls=%async_computation.8 | async-start | bytes 7864320 | tf_op jit(solution)/shard_map/reduce_scatter | solution.py:46
  14.4 0.9 copy-start.5
  14.4 61.6 %copy-start = (bf16[1,1,384,4096]{3,2,1,0:T(8,128)(2,1)S(1)}, bf16[1,1,384,4096]{3,2,1,0:T(8,128)(2,1)}, u32[]{:S(2)}) copy-start(bf16[1,1,384,4096]{3,2,1,0:T(8,128)(2,1)} %param.4) | copy-start | bytes 9437188
  14.4 61.6 %copy-start.1 = (f32[1,8,4096]{2,1,0:T(8,128)S(1)}, f32[1,8,4096]{2,1,0:T(8,128)}, u32[]{:S(2)}) copy-start(f32[1,8,4096]{2,1,0:T(8,128)} %param.5) | copy-start | bytes 393220
  14.4 61.6 %copy-start.4 = (s32[2]{0:T(128)S(1)}, s32[2]{0:T(128)}, u32[]{:S(2)}) copy-start(s32[2]{0:T(128)} %pad_add_fusion.g_ref.s_ref) | copy-start | bytes 28
  14.4 149.0 %reduce-scatter.5.cloned.1.call-start = ((), (), s32[]{:S(2)}) async-start(), calls=%async_computation.9 | async-start | bytes 1703936 | tf_op jit(solution)/shard_map/reduce_scatter | solution.py:46
  79.3 3.8 %collective-permute-start = (f32[8,64,256]{2,1,0:T(8,128)S(1)}, f32[8,64,256]{2,1,0:T(8,128)S(1)}, u32[]{:S(2)}, u32[]{:S(2)}) collective-permute-start(f32[8,64,256]{2,1,0:T(8,128)S(1)} %get-tuple-element.15), channel_id=1, source_target_pairs={{0,48},{48,0},{1,49},{49,1},{2,50},{50,2},{3,51},{51,3},{4,52},{52... | collective-permute-start | bytes 1572872 | tf_op jit(solution)/shard_map/ppermute | solution.py:50
  107.6 55.8 %copy-start.2 = (f32[8,4096]{1,0:T(8,128)S(1)}, f32[8,4096]{1,0:T(8,128)}, u32[]{:S(2)}) copy-start(f32[8,4096]{1,0:T(8,128)} %weight_ref.1) | copy-start | bytes 393220
  125.7 25.2 %all-to-all-start.5 = ((f32[32,16,256]{2,1,0:T(8,128)}), f32[32,16,256]{2,1,0:T(8,128)S(1)}, u32[]{:S(2)}, u32[]{:S(2)}) async-start(f32[32,16,256]{2,1,0:T(8,128)} %broadcast_in_dim.18), calls=%async_computation.6 | async-start | bytes 1048576 | tf_op jit(solution)/shard_map/all_to_all | solution.py:38
  150.9 7.9 %collective-permute-start.1 = (f32[8,64,256]{2,1,0:T(8,128)S(1)}, f32[8,64,256]{2,1,0:T(8,128)S(1)}, u32[]{:S(2)}, u32[]{:S(2)}) collective-permute-start(f32[8,64,256]{2,1,0:T(8,128)S(1)} %bitcast.31), channel_id=1, source_target_pairs={{0,48},{48,0},{1,49},{49,1},{2,50},{50,2},{3,51},{51,3},{4,52},{52... | collective-permute-start | bytes 1572872 | tf_op jit(solution)/shard_map/ppermute | solution.py:50
  163.4 0.9 copy-start.3
Sparse Core Ops, SparseCore 0:
  14.6 79.2 reduce-scatter.2
  107.8 55.5 reduce-scatter.4

commit v4 on v3

--- a/solution.py
+++ b/solution.py
@@ -13,10 +13,6 @@
 RANK, OWN, LANES = 64, 8, 128
 HIGHEST = lax.Precision.HIGHEST
 MIB = 2**20
-
-
-def full_dot(left, right):
-    return jnp.dot(left, right, precision=HIGHEST)
 
 
 def parts_of(value):
@@ -125,24 +121,56 @@
             keep_ref[k] = total[:, k * cols : (k + 1) * cols]
 
 
-def fold(blocks_ref, _, total_ref, __):
-    total = blocks_ref[0]
-    for i in range(1, blocks_ref.shape[0]):
-        total = total + blocks_ref[i]
-    total_ref[...] = total
-
-
-def finish(s_ref, mine_ref, other_ref, inverse_ref, left_ref, summed_ref, error_ref, weight_ref, q_ref, error_out, weight_out):
+def hand_on(_, __, ___):
+    pass
+
+
+def products(left, right):
+    a, b = parts_of(left), parts_of(right)
+    order = ((0, 0), (0, 1), (1, 0), (1, 1), (0, 2), (2, 0))
+    wide = jnp.concatenate([a[i] for i, _ in order], axis=1).astype(BF16)
+    return jnp.dot(wide, stacked([b[j] for _, j in order]), preferred_element_type=F32)
+
+
+def triangle(left_ref, own_ref, inverse_ref, hat_ref):
+    packed = left_ref[...]
+    both = products(packed.T, packed)
+    gram = both[:RANK, :RANK] + both[RANK:, RANK:]
+    row = lax.broadcasted_iota(jnp.int32, (RANK, RANK), 0)
+    diagonal = row == lax.broadcasted_iota(jnp.int32, (RANK, RANK), 1)
+    shift = 0.01 * (jnp.sum(jnp.where(diagonal, gram, 0.0)) / RANK + 1e-06)
+    eye = jnp.where(diagonal, 1.0, 0.0)
+    work = jnp.concatenate([gram + shift * eye, eye], axis=1)
+    below = lax.broadcasted_iota(jnp.int32, (RANK, 1), 0)
+    scale = jnp.zeros((RANK, 1), F32)
+    for k in range(RANK):
+        column, line = work[:, k : k + 1], work[k : k + 1]
+        pivot = line[:, k : k + 1]
+        scale = jnp.where(below == k, pivot, scale)
+        work = work - jnp.where(below > k, column / pivot, 0.0) * line
+    inverse = work[:, RANK:] * lax.rsqrt(scale)
+    inverse_ref[...] = inverse / (NY * NC)
+    hat_ref[...] = lax.dot_general(
+        own_ref[...], inverse, (((1,), (1,)), ((), ())), precision=HIGHEST, preferred_element_type=F32
+    )
+
+
+def apply(blocks_ref, inverse_ref, q_ref):
+    for k in range(blocks_ref.shape[0]):
+        q_ref[k] = products(inverse_ref[...], blocks_ref[k])
+
+
+def finish(s_ref, mine_ref, other_ref, left_ref, weight_ref, q_ref, approx_out, weight_out):
     step = pl.program_id(0)
     cols = mine_ref.shape[2]
 
     def run(blocks_ref):
         for k in range(blocks_ref.shape[0]):
             at = slice(k * cols, (k + 1) * cols)
-            block = jnp.dot(inverse_ref[...], blocks_ref[k], precision=HIGHEST, preferred_element_type=F32)
+            block = blocks_ref[k]
             q_ref[:, at] = block
-            approx = jnp.dot(left_ref[...], block, precision=HIGHEST, preferred_element_type=F32)
-            error_out[:, at] = summed_ref[:, at] + error_ref[:, at] - approx
+            approx = products(left_ref[...], block)
+            approx_out[:, at] = approx
             weight_out[:, at] = weight_ref[:, at] - 0.5 * approx
 
     pl.when(step == s_ref[1])(functools.partial(run, mine_ref))
@@ -207,42 +235,45 @@
         [array(NY, RANK, cols), array(NY, RANK, cols), array(OWN, RANK)],
         [pltpu.VMEM((2, 3 * RANK, half), BF16)],
     )(place, left, term, error)
-    blocks = exchange((keep + swap(send)).reshape(NY * NX, RANK // NX, cols), ("y", "x"))
+    half_sum = keep + swap(send)
+
+    inverse, left_hat = pl.pallas_call(
+        triangle,
+        out_shape=(array(RANK, RANK), array(OWN, RANK)),
+        compiler_params=pltpu.CompilerParams(vmem_limit_bytes=8 * MIB),
+        cost_estimate=pl.CostEstimate(flops=20 * 10**9, bytes_accessed=4 * half * LANES, transcendentals=RANK),
+    )(left, left_own)
 
     summed = scatter(wide.reshape(rows, width), "x")
-    vmem, anywhere = pl.BlockSpec(memory_space=pltpu.VMEM), pl.BlockSpec(memory_space=pl.ANY)
-    block, summed = pl.pallas_call(
-        fold,
-        out_shape=(array(RANK // NX, cols), array(*summed.shape)),
-        in_specs=[vmem, anywhere],
-        out_specs=(vmem, anywhere),
-        input_output_aliases={1: 1},
+    anywhere = pl.BlockSpec(memory_space=pl.ANY)
+    summed = pl.pallas_call(
+        hand_on,
+        out_shape=array(*summed.shape),
+        in_specs=[anywhere, anywhere],
+        out_specs=anywhere,
+        input_output_aliases={1: 0},
         compiler_params=pltpu.CompilerParams(vmem_limit_bytes=60 * MIB),
-    )(blocks, summed)
+    )(half_sum, summed)
     summed = scatter(summed, "z")
 
+    block = exchange(half_sum.reshape(NY * NX, RANK // NX, cols), ("y", "x")).sum(0)
     block = gathered(block, "z", NZ).sum(0)
-    mine = gathered(block, ("y", "x"), NY * NX).reshape(NY, RANK, cols)
+    mine = pl.pallas_call(
+        apply,
+        out_shape=array(NY, RANK, cols),
+        compiler_params=pltpu.CompilerParams(vmem_limit_bytes=8 * MIB),
+    )(gathered(block, ("y", "x"), NY * NX).reshape(NY, RANK, cols), inverse)
     other = swap(mine)
-
-    both = full_dot(left.T, left)
-    gram = both[:RANK, :RANK] + both[RANK:, RANK:]
-    shift = 0.01 * (jnp.trace(gram) / RANK + 1e-06)
-    eye = jnp.eye(RANK, dtype=F32)
-    lower = jnp.linalg.cholesky(gram + shift * eye)
-    inverse = lax.linalg.triangular_solve(lower, eye, left_side=True, lower=True)
-    left_hat = full_dot(left_own, inverse.T)
-
     side = pl.BlockSpec((OWN, width // 2), lambda i, _: (0, i))
-    q_turned, error_next, weight_next = call(
+    q_turned, approx, weight_next = call(
         finish,
         16,
         (2,),
-        [whole((NY, RANK, cols)), whole((NY, RANK, cols)), whole((RANK, RANK)), whole((OWN, RANK)), side, side, side],
+        [whole((NY, RANK, cols)), whole((NY, RANK, cols)), whole((OWN, RANK)), side],
         [pl.BlockSpec((RANK, width // 2), lambda i, _: (0, i)), side, side],
         [array(RANK, width), array(OWN, width), array(OWN, width)],
-    )(place, mine, other, inverse / (NY * NC), left_hat, summed, error, weight)
-    return (q_turned.T, error_next[None], weight_next)
+    )(place, mine, other, left_hat, weight)
+    return (q_turned.T, (summed + error - approx)[None], weight_next)
 
 
 def solution(mesh):

time: 178 us -> 172 us (0.966)
  waiting for transfers between devices: 12.8 us -> 37.7 us
  blocking collectives: 99.8 us -> 76.6 us
  other arithmetic: 13.7 us -> 3.16 us
  starting transfers between devices: 14.3 us -> 19.1 us
    all_to_all x5 -> x4, blocking collectives: 99.8 us -> 76.6 us  [exchange(): return lax.all_to_all(value, axes, 0, 0, tiled=True)]
    all_to_all x1 -> x2, waiting for transfers between devices: 6.28 us -> 22.4 us  [exchange(): return lax.all_to_all(value, axes, 0, 0, tiled=True)]
    another operation x5 -> x0, other arithmetic: 12.1 us -> none  [the longest x3 6.52 us: on_device(): lower = jnp.linalg.cholesky(gram + shift * eye)]
    reduce_scatter x2, waiting for transfers between devices: 4.63 us -> 11.5 us  [scatter(): return lax.psum_scatter(value, axis, scatter_dimension=0, tiled=True)]
    pallas_call x1 -> x3, Pallas kernels: 1.69 us -> 7.05 us  [the longest x1 6.6 us: on_device(): pl.pallas_call(triangle, out_shape=(array(RANK, RANK), array(OWN, RANK)),...]
    all_to_all x1 -> x2, starting transfers between devices: 10.4 us -> 15.2 us  [exchange(): return lax.all_to_all(value, axes, 0, 0, tiled=True)]
    pallas_call x1, Pallas kernels: 5.91 us -> 2.12 us  [on_device(): call(finish, 16, (2,), [whole((NY, RANK, cols)), whole((NY, RANK, cols)),...]
    ppermute x2, waiting for transfers between devices: 1.88 us -> 3.75 us  [swap(): return lax.ppermute(value, 'core', [(i, NC - 1 - i) for i in range(NC)])]
  transfers between devices with their start and end apart: 5 -> 6, of which waited for: 3 -> 6; matrix products, arithmetic and copies ran while one was open for 9% -> 1% of each run, Pallas kernels for 2% -> 7%
where the time goes in v4:
time: 172 us
  blocking collectives  76.6 us (45%)
  waiting for transfers between devices  37.7 us (22%)
  starting transfers between devices  19.1 us (11%)
  Pallas kernels  19.1 us (11%)
  between operations  14.2 us (8%)
  other arithmetic  3.16 us (2%)
  local copies, waits for them, and re-layouts  1.75 us (1%)
    all_to_all x4, blocking collectives, exchange(): return lax.all_to_all(value, axes, 0, 0, tiled=True)  76.6 us
    all_to_all x2, waiting for transfers between devices, exchange(): return lax.all_to_all(value, axes, 0, 0, tiled=True)  22.4 us
    all_to_all x2, starting transfers between devices, exchange(): return lax.all_to_all(value, axes, 0, 0, tiled=True)  15.2 us
    reduce_scatter x2, waiting for transfers between devices, scatter(): return lax.psum_scatter(value, axis, scatter_dimension=0, tiled=True)  11.5 us
    pallas_call x1, Pallas kernels, on_device(): pl.pallas_call(triangle, out_shape=(array(RANK, RANK), array(OWN, RANK)),...  6.6 us
    pallas_call x1, Pallas kernels, on_device(): call(prepare, 60, (2,), [pl.BlockSpec((half, width), lambda i, _: (i, 0))...  6.59 us
    ppermute x2, starting transfers between devices, swap(): return lax.ppermute(value, 'core', [(i, NC - 1 - i) for i in range(NC)])  3.84 us
    ppermute x2, waiting for transfers between devices, swap(): return lax.ppermute(value, 'core', [(i, NC - 1 - i) for i in range(NC)])  3.75 us
  transfers between devices with their start and end apart: 6, of which 6 were waited for; matrix products, arithmetic and copies ran while one was open for 1% of the time, Pallas kernels for 7%

profile of v4, /device:TPU:6, one launch (start us, length us, event | category | flops | bytes accessed | tf_op | source)
XLA Modules:
  0.0 171.5 jit_solution(14611993845239256675)
XLA Ops:
  7.2 0.0 reduce-scatter.3.cloned.1.call-start
  7.2 0.6 pad_add_fusion.g_ref.s_ref
  7.8 6.6 %shard_map.67 = (f32[4,12,8,4096]{3,2,1,0:T(8,128)}, f32[192,128]{1,0:T(8,128)}) custom-call(s32[2]{0:T(128)} %pad_add_fusion.g_ref.s_ref, bf16[384,4096]{1,0:T(8,128)(2,1)} %bitcast.14, f32[8,4096]{1,0:T(8,128)} %bitcast.17, f32[64,4096]{1,0:T(8,128)} %bitcast.22), custom_call_target="tpu_custom_call" | custom-call | tf_op jit(solution)/shard_map/pallas_call | solution.py:203
  14.4 0.0 copy-start.4
  14.4 0.0 copy-start
  14.4 0.0 copy-start.1
  14.4 0.0 copy-start.3
  14.4 0.0 reduce-scatter.3.cloned.1.call-update
  14.5 0.8 copy-done.4
  15.3 26.8 %all_to_all.30 = f32[24,8,128]{2,1,0:T(8,128)S(1)} all-to-all(f32[24,8,128]{2,1,0:T(8,128)S(1)} %bitcast.23), channel_id=1, replica_groups=mesh['y'=8,'core'=2,'z'=12,'x'=4] {'z','core'}, dimensions={0} | all-to-all | bytes 196608 | tf_op jit(solution)/shard_map/all_to_all | solution.py:34
  42.2 19.0 %all_to_all.31 = f32[32,8,128]{2,1,0:T(8,128)S(1)} all-to-all(f32[32,8,128]{2,1,0:T(8,128)S(1)} %broadcast_in_dim.10), channel_id=1, replica_groups=mesh['y'=8,'core'=2,'z'=12,'x'=4] {'y','x'}, dimensions={0} | all-to-all | bytes 262144 | tf_op jit(solution)/shard_map/all_to_all | solution.py:34
  61.2 14.8 %all_to_all.32 = f32[24,8,128]{2,1,0:T(8,128)S(1)} all-to-all(f32[24,8,128]{2,1,0:T(8,128)S(1)} %broadcast_in_dim.11), channel_id=1, replica_groups=mesh['y'=8,'core'=2,'z'=12,'x'=4] {'z','core'}, dimensions={0} | all-to-all | bytes 196608 | tf_op jit(solution)/shard_map/all_to_all | solution.py:34
  76.0 0.0 copy-done
  76.0 0.0 copy-done.1
  76.0 0.0 copy-done.3
  76.0 3.3 %shard_map.68 = (f32[8,64,256]{2,1,0:T(8,128)S(1)}, f32[8,64,256]{2,1,0:T(8,128)S(1)}, f32[8,64]{1,0:T(8,128)S(1)}) custom-call(s32[2]{0:T(128)S(1)} %copy-done.3, f32[192,128]{1,0:T(8,128)S(1)} %bitcast.19, bf16[384,4096]{1,0:T(8,128)(2,1)S(1)} %bitcast.15, f32[8,4096]{1,0:T(8,128)S(1)} %bitcast.18), custom_call_target="tpu_custom_call" | custom-call | tf_op jit(solution)/shard_map/pallas_call | solution.py:221
  79.3 1.9 %collective-permute-start = (f32[8,64,256]{2,1,0:T(8,128)S(1)}, f32[8,64,256]{2,1,0:T(8,128)S(1)}, u32[]{:S(2)}, u32[]{:S(2)}) collective-permute-start(f32[8,64,256]{2,1,0:T(8,128)S(1)} %get-tuple-element.15), channel_id=1, source_target_pairs={{0,48},{48,0},{1,49},{49,1},{2,50},{50,2},{3,51},{51,3},{4,52},{52... | collective-permute-start | bytes 1572872 | tf_op jit(solution)/shard_map/ppermute | solution.py:46
  81.3 1.9 %collective-permute-done = f32[8,64,256]{2,1,0:T(8,128)S(1)} collective-permute-done((f32[8,64,256]{2,1,0:T(8,128)S(1)}, f32[8,64,256]{2,1,0:T(8,128)S(1)}, u32[]{:S(2)}, u32[]{:S(2)}) %collective-permute-start) | collective-permute-done | bytes 524320 | tf_op jit(solution)/shard_map/ppermute | solution.py:46
  83.1 0.9 add.14._
  84.0 5.4 %all-to-all-start.3 = ((f32[32,16,256]{2,1,0:T(8,128)}), f32[32,16,256]{2,1,0:T(8,128)S(1)}, u32[]{:S(2)}, u32[]{:S(2)}) async-start(f32[32,16,256]{2,1,0:T(8,128)} %bitcast.7), calls=%async_computation.3 | async-start | bytes 1048576 | tf_op jit(solution)/shard_map/all_to_all | solution.py:34
  89.5 0.0 reduce-scatter.5.cloned.1.call-start
  89.5 3.3 %reduce-scatter.3.cloned.1.call-done.__ = f32[96,4096]{1,0:T(8,128)} async-done(((f32[384,4096]{1,0:T(8,128)}), f32[96,4096]{1,0:T(8,128)}) %reduce-scatter.3.cloned.1.call-update) | async-done | bytes 1572880 | tf_op jit(solution)/shard_map/reduce_scatter | solution.py:42
  92.8 0.0 reduce-scatter.5.cloned.1.call-update
  92.9 14.1 %all-to-all-done.3 = f32[32,16,256]{2,1,0:T(8,128)S(1)} async-done(((f32[32,16,256]{2,1,0:T(8,128)}), f32[32,16,256]{2,1,0:T(8,128)S(1)}, u32[]{:S(2)}, u32[]{:S(2)}) %all-to-all-start.3) | async-done | bytes 524320 | tf_op jit(solution)/shard_map/all_to_all | solution.py:34
  107.0 16.0 %all_to_all.33 = f32[12,16,256]{2,1,0:T(8,128)S(1)} all-to-all(f32[12,16,256]{2,1,0:T(8,128)S(1)} %broadcast_in_dim.12), channel_id=1, replica_groups=mesh['y'=8,'core'=2,'z'=12,'x'=4] {'z'}, dimensions={0} | all-to-all | bytes 393216 | tf_op jit(solution)/shard_map/all_to_all | solution.py:34
  123.0 0.9 broadcast_in_dim.13
  123.9 9.7 %all-to-all-start.5 = ((f32[32,16,256]{2,1,0:T(8,128)}), f32[32,16,256]{2,1,0:T(8,128)S(1)}, u32[]{:S(2)}, u32[]{:S(2)}) async-start(f32[32,16,256]{2,1,0:T(8,128)} %broadcast_in_dim.13), calls=%async_computation.5 | async-start | bytes 1048576 | tf_op jit(solution)/shard_map/all_to_all | solution.py:34
  133.6 0.0 copy-start.2
  133.6 6.6 %shard_map.69 = (f32[64,64]{1,0:T(8,128)S(1)}, f32[8,64]{1,0:T(8,128)S(1)}) custom-call(f32[192,128]{1,0:T(8,128)S(1)} %bitcast.20, f32[8,64]{1,0:T(8,128)S(1)} %get-tuple-element.16.own_ref), custom_call_target="tpu_custom_call" | custom-call | flops 20000000000 | bytes 98304 | tf_op jit(solution)/shard_map/pallas_call | solution.py:240
  140.2 8.3 %all-to-all-done.5 = f32[32,16,256]{2,1,0:T(8,128)S(1)} async-done(((f32[32,16,256]{2,1,0:T(8,128)}), f32[32,16,256]{2,1,0:T(8,128)S(1)}, u32[]{:S(2)}, u32[]{:S(2)}) %all-to-all-start.5) | async-done | bytes 524320 | tf_op jit(solution)/shard_map/all_to_all | solution.py:34
  148.6 0.4 shard_map.70.mine_ref
  149.0 1.9 %collective-permute-start.1 = (f32[8,64,256]{2,1,0:T(8,128)S(1)}, f32[8,64,256]{2,1,0:T(8,128)S(1)}, u32[]{:S(2)}, u32[]{:S(2)}) collective-permute-start(f32[8,64,256]{2,1,0:T(8,128)S(1)} %shard_map.70.mine_ref), channel_id=1, source_target_pairs={{0,48},{48,0},{1,49},{49,1},{2,50},{50,2},{3,51},{51,3},{4,52},{52... | collective-permute-start | bytes 1572872 | tf_op jit(solution)/shard_map/ppermute | solution.py:46
  150.9 1.9 %collective-permute-done.1.other_ref = f32[8,64,256]{2,1,0:T(8,128)S(1)} collective-permute-done((f32[8,64,256]{2,1,0:T(8,128)S(1)}, f32[8,64,256]{2,1,0:T(8,128)S(1)}, u32[]{:S(2)}, u32[]{:S(2)}) %collective-permute-start.1) | collective-permute-done | bytes 524320 | tf_op jit(solution)/shard_map/ppermute | solution.py:46
  152.8 0.0 copy-done.2
  152.8 2.1 %shard_map.71 = (f32[64,4096]{1,0:T(8,128)}, f32[8,4096]{1,0:T(8,128)S(1)}, f32[8,4096]{1,0:T(8,128)}) custom-call(s32[2]{0:T(128)S(1)} %copy-done.3, f32[8,64,256]{2,1,0:T(8,128)S(1)} %shard_map.70.mine_ref, f32[8,64,256]{2,1,0:T(8,128)S(1)} %collective-permute-done.1.other_ref, f32[8,64]{1,0:T(8,128)S(1)} %get-tuple-element.18.left_ref, ...), custom_call_target="tpu_custom_call" | custom-call | tf_op jit(solution)/shard_map/pallas_call | solution.py:268
  154.9 8.2 %reduce-scatter.5.cloned.1.call-done = f32[8,4096]{1,0:T(8,128)} async-done(((f32[96,4096]{1,0:T(8,128)}), f32[8,4096]{1,0:T(8,128)}) %reduce-scatter.5.cloned.1.call-update) | async-done | bytes 131088 | tf_op jit(solution)/shard_map/reduce_scatter | solution.py:42
  163.1 1.6 subtract_bitcast_fusion
  (8 shorter events, 0.2 us)
Async XLA Ops:
  7.2 85.7 %reduce-scatter.3.cloned.1.call-start = ((), (), s32[]{:S(2)}) async-start(), calls=%async_computation.8 | async-start | bytes 7864320 | tf_op jit(solution)/shard_map/reduce_scatter | solution.py:42
  14.4 0.9 copy-start.4
  14.4 61.6 %copy-start = (bf16[1,1,384,4096]{3,2,1,0:T(8,128)(2,1)S(1)}, bf16[1,1,384,4096]{3,2,1,0:T(8,128)(2,1)}, u32[]{:S(2)}) copy-start(bf16[1,1,384,4096]{3,2,1,0:T(8,128)(2,1)} %param.4) | copy-start | bytes 9437188
  14.4 61.6 %copy-start.1 = (f32[1,8,4096]{2,1,0:T(8,128)S(1)}, f32[1,8,4096]{2,1,0:T(8,128)}, u32[]{:S(2)}) copy-start(f32[1,8,4096]{2,1,0:T(8,128)} %param.5) | copy-start | bytes 393220
  14.4 61.6 %copy-start.3 = (s32[2]{0:T(128)S(1)}, s32[2]{0:T(128)}, u32[]{:S(2)}) copy-start(s32[2]{0:T(128)} %pad_add_fusion.g_ref.s_ref) | copy-start | bytes 28
  79.3 3.8 %collective-permute-start = (f32[8,64,256]{2,1,0:T(8,128)S(1)}, f32[8,64,256]{2,1,0:T(8,128)S(1)}, u32[]{:S(2)}, u32[]{:S(2)}) collective-permute-start(f32[8,64,256]{2,1,0:T(8,128)S(1)} %get-tuple-element.15), channel_id=1, source_target_pairs={{0,48},{48,0},{1,49},{49,1},{2,50},{50,2},{3,51},{51,3},{4,52},{52... | collective-permute-start | bytes 1572872 | tf_op jit(solution)/shard_map/ppermute | solution.py:46
  84.0 22.9 %all-to-all-start.3 = ((f32[32,16,256]{2,1,0:T(8,128)}), f32[32,16,256]{2,1,0:T(8,128)S(1)}, u32[]{:S(2)}, u32[]{:S(2)}) async-start(f32[32,16,256]{2,1,0:T(8,128)} %bitcast.7), calls=%async_computation.3 | async-start | bytes 1048576 | tf_op jit(solution)/shard_map/all_to_all | solution.py:34
  89.5 73.6 %reduce-scatter.5.cloned.1.call-start = ((), (), s32[]{:S(2)}) async-start(), calls=%async_computation.9 | async-start | bytes 1703936 | tf_op jit(solution)/shard_map/reduce_scatter | solution.py:42
  123.9 24.7 %all-to-all-start.5 = ((f32[32,16,256]{2,1,0:T(8,128)}), f32[32,16,256]{2,1,0:T(8,128)S(1)}, u32[]{:S(2)}, u32[]{:S(2)}) async-start(f32[32,16,256]{2,1,0:T(8,128)} %broadcast_in_dim.13), calls=%async_computation.5 | async-start | bytes 1048576 | tf_op jit(solution)/shard_map/all_to_all | solution.py:34
  133.6 19.2 %copy-start.2 = (f32[8,4096]{1,0:T(8,128)S(1)}, f32[8,4096]{1,0:T(8,128)}, u32[]{:S(2)}) copy-start(f32[8,4096]{1,0:T(8,128)} %weight_ref.1) | copy-start | bytes 393220
  149.0 3.8 %collective-permute-start.1 = (f32[8,64,256]{2,1,0:T(8,128)S(1)}, f32[8,64,256]{2,1,0:T(8,128)S(1)}, u32[]{:S(2)}, u32[]{:S(2)}) collective-permute-start(f32[8,64,256]{2,1,0:T(8,128)S(1)} %shard_map.70.mine_ref), channel_id=1, source_target_pairs={{0,48},{48,0},{1,49},{49,1},{2,50},{50,2},{3,51},{51,3},{4,52},{52... | collective-permute-start | bytes 1572872 | tf_op jit(solution)/shard_map/ppermute | solution.py:46
Sparse Core Ops, SparseCore 0:
  14.6 78.2 reduce-scatter.2
  96.0 67.0 reduce-scatter.4

commit v5 on v4

--- a/solution.py
+++ b/solution.py
@@ -13,6 +13,7 @@
 RANK, OWN, LANES = 64, 8, 128
 HIGHEST = lax.Precision.HIGHEST
 MIB = 2**20
+PAIRS = ((0, 0), (0, 1), (1, 0), (1, 1), (0, 2), (2, 0))
 
 
 def parts_of(value):
@@ -51,7 +52,15 @@
     return low, pl.multiple_of(jnp.where(low, g, g - n_tiles) * OWN, OWN)
 
 
-def prepare(g_ref, term_ref, error_ref, q_ref, wide_ref, left_ref, parts):
+def widen(term_ref, wide_ref):
+    block = term_ref[...].astype(F32)
+    for z in range(wide_ref.shape[1]):
+        for x in range(NX):
+            at = (z * NX + x) * OWN
+            wide_ref[x, z] = block[at : at + OWN]
+
+
+def left_terms(term_ref, error_ref, q_ref, left_ref, parts):
     step = pl.program_id(0)
     rows = term_ref.shape[0]
 
@@ -60,12 +69,7 @@
         for i, part in enumerate(parts_of(q_ref[...])):
             parts[i * RANK : (i + 1) * RANK] = part.astype(BF16)
 
-    block = term_ref[...]
-    for z in range(rows // (NX * OWN)):
-        band = block[z * NX * OWN : (z + 1) * NX * OWN].astype(F32)
-        for x in range(NX):
-            wide_ref[x, z] = band[x * OWN : (x + 1) * OWN]
-    product = dot_nt(block, parts[...])
+    product = dot_nt(term_ref[...], parts[...])
     left = product[:, :RANK] + product[:, RANK : 2 * RANK] + product[:, 2 * RANK :]
 
     @pl.when(step == 0)
@@ -82,13 +86,13 @@
         own = own + cross[OWN : 2 * OWN, RANK : 2 * RANK]
         own = own + cross[OWN : 2 * OWN, :RANK] + cross[:OWN, RANK : 2 * RANK]
         own = own + cross[:OWN, :RANK]
-        first, at = own_place(g_ref[0], rows // OWN)
+        first, at = own_place(lax.axis_index("z") * NX + lax.axis_index("x"), rows // OWN)
         none = jnp.zeros_like(own)
         pair = jnp.concatenate([jnp.where(first, own, none), jnp.where(first, none, own)], axis=1)
         left_ref[pl.ds(at, OWN), :] += pair
 
 
-def right_terms(s_ref, left_ref, term_ref, error_ref, send_ref, keep_ref, own_ref, parts):
+def right_terms(s_ref, left_ref, term_ref, error_ref, send_ref, keep_ref, own_ref, parts, own_parts):
     step = pl.program_id(0)
     half = term_ref.shape[0] // 2
     first, at = own_place(s_ref[0], half // OWN)
@@ -100,14 +104,16 @@
             for j, part in enumerate(parts_of(turned[i * RANK : (i + 1) * RANK])):
                 parts[i, j * RANK : (j + 1) * RANK] = part.astype(BF16)
         pair = left_ref[pl.ds(at, OWN), :]
-        own_ref[...] = jnp.where(first, pair[:, :RANK], pair[:, RANK:])
+        own = jnp.where(first, pair[:, :RANK], pair[:, RANK:])
+        own_ref[...] = own
+        cut = parts_of(own)
+        own_parts[...] = jnp.concatenate([cut[i] for i, _ in PAIRS], axis=0).T.astype(BF16)
 
     total = jnp.dot(parts[0], term_ref[:half], preferred_element_type=F32)
     total = total + jnp.dot(parts[1], term_ref[half:], preferred_element_type=F32)
     total = total[:RANK] + total[RANK : 2 * RANK] + total[2 * RANK :]
-    total = total + lax.dot_general(
-        own_ref[...], error_ref[...], (((0,), (0,)), ((), ())), precision=HIGHEST, preferred_element_type=F32
-    )
+    cut = parts_of(error_ref[...])
+    total = total + jnp.dot(own_parts[...], stacked([cut[j] for _, j in PAIRS]), preferred_element_type=F32)
     count, cols = send_ref.shape[0], send_ref.shape[2]
 
     @pl.when(step < 2)
@@ -127,9 +133,8 @@
 
 def products(left, right):
     a, b = parts_of(left), parts_of(right)
-    order = ((0, 0), (0, 1), (1, 0), (1, 1), (0, 2), (2, 0))
-    wide = jnp.concatenate([a[i] for i, _ in order], axis=1).astype(BF16)
-    return jnp.dot(wide, stacked([b[j] for _, j in order]), preferred_element_type=F32)
+    wide = jnp.concatenate([a[i] for i, _ in PAIRS], axis=1).astype(BF16)
+    return jnp.dot(wide, stacked([b[j] for _, j in PAIRS]), preferred_element_type=F32)
 
 
 def triangle(left_ref, own_ref, inverse_ref, hat_ref):
@@ -200,19 +205,23 @@
     core = lax.axis_index("core")
     place = jnp.stack([lax.axis_index("z") * NX + lax.axis_index("x"), core]).astype(jnp.int32)
 
-    wide, left = call(
-        prepare,
-        60,
-        (2,),
-        [
-            pl.BlockSpec((half, width), lambda i, _: (i, 0)),
-            whole((OWN, width)),
-            whole((RANK, width)),
-        ],
-        [pl.BlockSpec((NX, NZ // 2, OWN, width), lambda i, _: (0, i, 0, 0)), whole((half, LANES))],
-        [array(NX, NZ, OWN, width), array(half, LANES)],
-        [pltpu.VMEM((3 * RANK, width), BF16)],
-    )(place, term, error, q_prev.T)
+    wide = pl.pallas_call(
+        widen,
+        out_shape=array(NX, NZ, OWN, width),
+        grid=(NZ // 2,),
+        in_specs=[pl.BlockSpec((2 * NX * OWN, width), lambda i: (i, 0))],
+        out_specs=pl.BlockSpec((NX, 2, OWN, width), lambda i: (0, i, 0, 0)),
+        compiler_params=pltpu.CompilerParams(vmem_limit_bytes=60 * MIB),
+    )(term)
+    left = pl.pallas_call(
+        left_terms,
+        out_shape=array(half, LANES),
+        grid=(2,),
+        in_specs=[pl.BlockSpec((half, width), lambda i: (i, 0)), whole((OWN, width)), whole((RANK, width))],
+        out_specs=whole((half, LANES)),
+        scratch_shapes=[pltpu.VMEM((3 * RANK, width), BF16)],
+        compiler_params=pltpu.CompilerParams(vmem_limit_bytes=60 * MIB),
+    )(term, error, q_prev.T)
 
     tile = exchange(left.reshape(NZ * NC, half // (NZ * NC), LANES), ("z", "core")).sum(0)
     tile = gathered(tile, ("y", "x"), NY * NX).sum(0)
@@ -233,7 +242,7 @@
             whole((OWN, RANK)),
         ],
         [array(NY, RANK, cols), array(NY, RANK, cols), array(OWN, RANK)],
-        [pltpu.VMEM((2, 3 * RANK, half), BF16)],
+        [pltpu.VMEM((2, 3 * RANK, half), BF16), pltpu.VMEM((RANK, len(PAIRS) * OWN), BF16)],
     )(place, left, term, error)
     half_sum = keep + swap(send)
 

time: 172 us -> 170 us (0.988)
  blocking collectives: 76.6 us -> 63 us
  waiting for transfers between devices: 37.7 us -> 46.9 us
  Pallas kernels: 19.1 us -> 22.5 us
    all_to_all x4 -> x3, blocking collectives: 76.6 us -> 63 us  [exchange(): return lax.all_to_all(value, axes, 0, 0, tiled=True)]
    all_to_all x2 -> x3, waiting for transfers between devices: 22.4 us -> 35.6 us  [exchange(): return lax.all_to_all(value, axes, 0, 0, tiled=True)]
    reduce_scatter x2, waiting for transfers between devices: 11.5 us -> 6.89 us  [scatter(): return lax.psum_scatter(value, axis, scatter_dimension=0, tiled=True)]
    pallas_call x1 -> x2, Pallas kernels: 6.59 us -> 10.7 us  [the longest x1 5.77 us: on_device(): pl.pallas_call(widen, out_shape=array(NX, NZ, OWN, width), grid=(NZ // 2,...]
    all_to_all x2 -> x3, starting transfers between devices: 15.2 us -> 14.1 us  [exchange(): return lax.all_to_all(value, axes, 0, 0, tiled=True)]
  transfers between devices with their start and end apart: 6 -> 7, of which waited for: 6 -> 6; matrix products, arithmetic and copies ran while one was open for 1% -> 2% of each run, Pallas kernels for 7% -> 10%
where the time goes in v5:
time: 170 us; the launch traced here: 169 us
  blocking collectives  63 us (37%)
  waiting for transfers between devices  46.9 us (28%)
  Pallas kernels  22.5 us (13%)
  starting transfers between devices  18.1 us (11%)
  between operations  14.2 us (8%)
  other arithmetic  2.64 us (2%)
    all_to_all x3, blocking collectives, exchange(): return lax.all_to_all(value, axes, 0, 0, tiled=True)  63 us
    all_to_all x3, waiting for transfers between devices, exchange(): return lax.all_to_all(value, axes, 0, 0, tiled=True)  35.6 us
    all_to_all x3, starting transfers between devices, exchange(): return lax.all_to_all(value, axes, 0, 0, tiled=True)  14.1 us
    reduce_scatter x2, waiting for transfers between devices, scatter(): return lax.psum_scatter(value, axis, scatter_dimension=0, tiled=True)  6.89 us
    pallas_call x1, Pallas kernels, on_device(): pl.pallas_call(triangle, out_shape=(array(RANK, RANK), array(OWN, RANK)),...  6.6 us
    pallas_call x1, Pallas kernels, on_device(): pl.pallas_call(widen, out_shape=array(NX, NZ, OWN, width), grid=(NZ // 2,...  5.77 us
    pallas_call x1, Pallas kernels, on_device(): pl.pallas_call(left_terms, out_shape=array(half, LANES), grid=(2,), in_sp...  4.89 us
    ppermute x2, starting transfers between devices, swap(): return lax.ppermute(value, 'core', [(i, NC - 1 - i) for i in range(NC)])  3.84 us
  transfers between devices with their start and end apart: 7, of which 6 were waited for; matrix products, arithmetic and copies ran while one was open for 2% of the time, Pallas kernels for 10%

profile of v5, /device:TPU:6, one launch (start us, length us, event | category | flops | bytes accessed | tf_op | source)
XLA Modules:
  0.0 168.8 jit_solution(8398580197841808767)
XLA Ops:
  7.2 0.0 reduce-scatter.3.cloned.1.call-start
  7.2 5.8 %shard_map.72 = f32[4,12,8,4096]{3,2,1,0:T(8,128)} custom-call(bf16[384,4096]{1,0:T(8,128)(2,1)} %bitcast.14), custom_call_target="tpu_custom_call" | custom-call | tf_op jit(solution)/shard_map/pallas_call | solution.py:208
  13.0 0.0 reduce-scatter.3.cloned.1.call-update
  13.0 0.0 copy-start
  13.0 0.0 copy-start.1
  13.0 4.9 %shard_map.67 = f32[192,128]{1,0:T(8,128)} custom-call(bf16[384,4096]{1,0:T(8,128)(2,1)} %bitcast.15, f32[8,4096]{1,0:T(8,128)} %bitcast.18, f32[64,4096]{1,0:T(8,128)} %bitcast.23), custom_call_target="tpu_custom_call" | custom-call | tf_op jit(solution)/shard_map/pallas_call | solution.py:216
  17.9 26.9 %all_to_all.30 = f32[24,8,128]{2,1,0:T(8,128)S(1)} all-to-all(f32[24,8,128]{2,1,0:T(8,128)} %bitcast.24), channel_id=1, replica_groups=mesh['y'=8,'core'=2,'z'=12,'x'=4] {'z','core'}, dimensions={0} | all-to-all | bytes 196608 | tf_op jit(solution)/shard_map/all_to_all | solution.py:35
  44.9 19.0 %all_to_all.31 = f32[32,8,128]{2,1,0:T(8,128)S(1)} all-to-all(f32[32,8,128]{2,1,0:T(8,128)S(1)} %broadcast_in_dim.10), channel_id=1, replica_groups=mesh['y'=8,'core'=2,'z'=12,'x'=4] {'y','x'}, dimensions={0} | all-to-all | bytes 262144 | tf_op jit(solution)/shard_map/all_to_all | solution.py:35
  63.9 0.7 broadcast_in_dim.11
  64.5 3.8 %all-to-all-start.2 = ((f32[24,8,128]{2,1,0:T(8,128)}), f32[24,8,128]{2,1,0:T(8,128)S(1)}, u32[]{:S(2)}, u32[]{:S(2)}) async-start(f32[24,8,128]{2,1,0:T(8,128)} %broadcast_in_dim.11), calls=%async_computation.2 | async-start | bytes 196608 | tf_op jit(solution)/shard_map/all_to_all | solution.py:35
  68.4 0.1 pad_add_fusion.s_ref
  68.4 11.4 %all-to-all-done.2 = f32[24,8,128]{2,1,0:T(8,128)S(1)} async-done(((f32[24,8,128]{2,1,0:T(8,128)}), f32[24,8,128]{2,1,0:T(8,128)S(1)}, u32[]{:S(2)}, u32[]{:S(2)}) %all-to-all-start.2) | async-done | bytes 98336 | tf_op jit(solution)/shard_map/all_to_all | solution.py:35
  79.9 0.0 copy-done
  79.9 0.0 copy-done.1
  79.9 2.7 %shard_map.68 = (f32[8,64,256]{2,1,0:T(8,128)S(1)}, f32[8,64,256]{2,1,0:T(8,128)S(1)}, f32[8,64]{1,0:T(8,128)S(1)}) custom-call(s32[2]{0:T(128)S(1)} %pad_add_fusion.s_ref, f32[192,128]{1,0:T(8,128)S(1)} %bitcast.20, bf16[384,4096]{1,0:T(8,128)(2,1)S(1)} %bitcast.16, f32[8,4096]{1,0:T(8,128)S(1)} %bitcast.19), custom_call_target="tpu_custom_call" | custom-call | tf_op jit(solution)/shard_map/pallas_call | solution.py:230
  82.6 1.9 %collective-permute-start = (f32[8,64,256]{2,1,0:T(8,128)S(1)}, f32[8,64,256]{2,1,0:T(8,128)S(1)}, u32[]{:S(2)}, u32[]{:S(2)}) collective-permute-start(f32[8,64,256]{2,1,0:T(8,128)S(1)} %get-tuple-element.12), channel_id=1, source_target_pairs={{0,48},{48,0},{1,49},{49,1},{2,50},{50,2},{3,51},{51,3},{4,52},{52... | collective-permute-start | bytes 1572872 | tf_op jit(solution)/shard_map/ppermute | solution.py:47
  84.5 1.9 %collective-permute-done = f32[8,64,256]{2,1,0:T(8,128)S(1)} collective-permute-done((f32[8,64,256]{2,1,0:T(8,128)S(1)}, f32[8,64,256]{2,1,0:T(8,128)S(1)}, u32[]{:S(2)}, u32[]{:S(2)}) %collective-permute-start) | collective-permute-done | bytes 524320 | tf_op jit(solution)/shard_map/ppermute | solution.py:47
  86.4 0.9 add.14._
  87.2 5.3 %all-to-all-start.3 = ((f32[32,16,256]{2,1,0:T(8,128)}), f32[32,16,256]{2,1,0:T(8,128)S(1)}, u32[]{:S(2)}, u32[]{:S(2)}) async-start(f32[32,16,256]{2,1,0:T(8,128)} %bitcast.7), calls=%async_computation.3 | async-start | bytes 1048576 | tf_op jit(solution)/shard_map/all_to_all | solution.py:35
  92.6 0.0 reduce-scatter.5.cloned.1.call-start
  92.6 0.0 reduce-scatter.3.cloned.1.call-done.__
  92.7 0.7 reduce-scatter.5.cloned.1.call-update
  93.3 16.7 %all-to-all-done.3 = f32[32,16,256]{2,1,0:T(8,128)S(1)} async-done(((f32[32,16,256]{2,1,0:T(8,128)}), f32[32,16,256]{2,1,0:T(8,128)S(1)}, u32[]{:S(2)}, u32[]{:S(2)}) %all-to-all-start.3) | async-done | bytes 524320 | tf_op jit(solution)/shard_map/all_to_all | solution.py:35
  110.1 17.1 %all_to_all.32 = f32[12,16,256]{2,1,0:T(8,128)S(1)} all-to-all(f32[12,16,256]{2,1,0:T(8,128)S(1)} %broadcast_in_dim.12), channel_id=1, replica_groups=mesh['y'=8,'core'=2,'z'=12,'x'=4] {'z'}, dimensions={0} | all-to-all | bytes 393216 | tf_op jit(solution)/shard_map/all_to_all | solution.py:35
  127.2 0.9 broadcast_in_dim.13
  128.1 5.0 %all-to-all-start.5 = ((f32[32,16,256]{2,1,0:T(8,128)}), f32[32,16,256]{2,1,0:T(8,128)S(1)}, u32[]{:S(2)}, u32[]{:S(2)}) async-start(f32[32,16,256]{2,1,0:T(8,128)} %broadcast_in_dim.13), calls=%async_computation.5 | async-start | bytes 1048576 | tf_op jit(solution)/shard_map/all_to_all | solution.py:35
  133.1 0.0 copy-start.2
  133.1 6.6 %shard_map.69 = (f32[64,64]{1,0:T(8,128)S(1)}, f32[8,64]{1,0:T(8,128)S(1)}) custom-call(f32[192,128]{1,0:T(8,128)S(1)} %bitcast.21, f32[8,64]{1,0:T(8,128)S(1)} %get-tuple-element.13.own_ref), custom_call_target="tpu_custom_call" | custom-call | flops 20000000000 | bytes 98304 | tf_op jit(solution)/shard_map/pallas_call | solution.py:249
  139.7 7.4 %all-to-all-done.5 = f32[32,16,256]{2,1,0:T(8,128)S(1)} async-done(((f32[32,16,256]{2,1,0:T(8,128)}), f32[32,16,256]{2,1,0:T(8,128)S(1)}, u32[]{:S(2)}, u32[]{:S(2)}) %all-to-all-start.5) | async-done | bytes 524320 | tf_op jit(solution)/shard_map/all_to_all | solution.py:35
  147.1 0.4 shard_map.70.mine_ref
  147.6 1.9 %collective-permute-start.1 = (f32[8,64,256]{2,1,0:T(8,128)S(1)}, f32[8,64,256]{2,1,0:T(8,128)S(1)}, u32[]{:S(2)}, u32[]{:S(2)}) collective-permute-start(f32[8,64,256]{2,1,0:T(8,128)S(1)} %shard_map.70.mine_ref), channel_id=1, source_target_pairs={{0,48},{48,0},{1,49},{49,1},{2,50},{50,2},{3,51},{51,3},{4,52},{52... | collective-permute-start | bytes 1572872 | tf_op jit(solution)/shard_map/ppermute | solution.py:47
  149.5 1.9 %collective-permute-done.1.other_ref = f32[8,64,256]{2,1,0:T(8,128)S(1)} collective-permute-done((f32[8,64,256]{2,1,0:T(8,128)S(1)}, f32[8,64,256]{2,1,0:T(8,128)S(1)}, u32[]{:S(2)}, u32[]{:S(2)}) %collective-permute-start.1) | collective-permute-done | bytes 524320 | tf_op jit(solution)/shard_map/ppermute | solution.py:47
  151.4 0.0 copy-done.2
  151.4 2.1 %shard_map.71 = (f32[64,4096]{1,0:T(8,128)}, f32[8,4096]{1,0:T(8,128)S(1)}, f32[8,4096]{1,0:T(8,128)}) custom-call(s32[2]{0:T(128)S(1)} %pad_add_fusion.s_ref, f32[8,64,256]{2,1,0:T(8,128)S(1)} %shard_map.70.mine_ref, f32[8,64,256]{2,1,0:T(8,128)S(1)} %collective-permute-done.1.other_ref, f32[8,64]{1,0:T(8,128)S(1)} %get-tuple-element.15.left_ref, ...), custom_call_target="tpu_custom_call" | custom-call | tf_op jit(solution)/shard_map/pallas_call | solution.py:277
  153.5 6.9 %reduce-scatter.5.cloned.1.call-done = f32[8,4096]{1,0:T(8,128)} async-done(((f32[96,4096]{1,0:T(8,128)}), f32[8,4096]{1,0:T(8,128)}) %reduce-scatter.5.cloned.1.call-update) | async-done | bytes 131088 | tf_op jit(solution)/shard_map/reduce_scatter | solution.py:43
  160.4 1.6 subtract_bitcast_fusion
  (7 shorter events, 0.2 us)
Async XLA Ops:
  7.2 85.5 %reduce-scatter.3.cloned.1.call-start = ((), (), s32[]{:S(2)}) async-start(), calls=%async_computation.8 | async-start | bytes 7864320 | tf_op jit(solution)/shard_map/reduce_scatter | solution.py:43
  13.0 66.8 %copy-start = (bf16[1,1,384,4096]{3,2,1,0:T(8,128)(2,1)S(1)}, bf16[1,1,384,4096]{3,2,1,0:T(8,128)(2,1)}, u32[]{:S(2)}) copy-start(bf16[1,1,384,4096]{3,2,1,0:T(8,128)(2,1)} %param.4) | copy-start | bytes 9437188
  13.0 66.8 %copy-start.1 = (f32[1,8,4096]{2,1,0:T(8,128)S(1)}, f32[1,8,4096]{2,1,0:T(8,128)}, u32[]{:S(2)}) copy-start(f32[1,8,4096]{2,1,0:T(8,128)} %param.5) | copy-start | bytes 393220
  64.5 15.3 %all-to-all-start.2 = ((f32[24,8,128]{2,1,0:T(8,128)}), f32[24,8,128]{2,1,0:T(8,128)S(1)}, u32[]{:S(2)}, u32[]{:S(2)}) async-start(f32[24,8,128]{2,1,0:T(8,128)} %broadcast_in_dim.11), calls=%async_computation.2 | async-start | bytes 196608 | tf_op jit(solution)/shard_map/all_to_all | solution.py:35
  82.6 3.8 %collective-permute-start = (f32[8,64,256]{2,1,0:T(8,128)S(1)}, f32[8,64,256]{2,1,0:T(8,128)S(1)}, u32[]{:S(2)}, u32[]{:S(2)}) collective-permute-start(f32[8,64,256]{2,1,0:T(8,128)S(1)} %get-tuple-element.12), channel_id=1, source_target_pairs={{0,48},{48,0},{1,49},{49,1},{2,50},{50,2},{3,51},{51,3},{4,52},{52... | collective-permute-start | bytes 1572872 | tf_op jit(solution)/shard_map/ppermute | solution.py:47
  87.2 22.8 %all-to-all-start.3 = ((f32[32,16,256]{2,1,0:T(8,128)}), f32[32,16,256]{2,1,0:T(8,128)S(1)}, u32[]{:S(2)}, u32[]{:S(2)}) async-start(f32[32,16,256]{2,1,0:T(8,128)} %bitcast.7), calls=%async_computation.3 | async-start | bytes 1048576 | tf_op jit(solution)/shard_map/all_to_all | solution.py:35
  92.6 67.8 %reduce-scatter.5.cloned.1.call-start = ((), (), s32[]{:S(2)}) async-start(), calls=%async_computation.9 | async-start | bytes 1703936 | tf_op jit(solution)/shard_map/reduce_scatter | solution.py:43
  128.1 19.0 %all-to-all-start.5 = ((f32[32,16,256]{2,1,0:T(8,128)}), f32[32,16,256]{2,1,0:T(8,128)S(1)}, u32[]{:S(2)}, u32[]{:S(2)}) async-start(f32[32,16,256]{2,1,0:T(8,128)} %broadcast_in_dim.13), calls=%async_computation.5 | async-start | bytes 1048576 | tf_op jit(solution)/shard_map/all_to_all | solution.py:35
  133.1 18.3 %copy-start.2 = (f32[8,4096]{1,0:T(8,128)S(1)}, f32[8,4096]{1,0:T(8,128)}, u32[]{:S(2)}) copy-start(f32[8,4096]{1,0:T(8,128)} %weight_ref.1) | copy-start | bytes 393220
  147.6 3.8 %collective-permute-start.1 = (f32[8,64,256]{2,1,0:T(8,128)S(1)}, f32[8,64,256]{2,1,0:T(8,128)S(1)}, u32[]{:S(2)}, u32[]{:S(2)}) collective-permute-start(f32[8,64,256]{2,1,0:T(8,128)S(1)} %shard_map.70.mine_ref), channel_id=1, source_target_pairs={{0,48},{48,0},{1,49},{49,1},{2,50},{50,2},{3,51},{51,3},{4,52},{52... | collective-permute-start | bytes 1572872 | tf_op jit(solution)/shard_map/ppermute | solution.py:47
Sparse Core Ops, SparseCore 0:
  13.1 78.2 reduce-scatter.2
  96.5 63.8 reduce-scatter.4

commit v6 on v5

--- a/solution.py
+++ b/solution.py
@@ -52,12 +52,24 @@
     return low, pl.multiple_of(jnp.where(low, g, g - n_tiles) * OWN, OWN)
 
 
-def widen(term_ref, wide_ref):
-    block = term_ref[...].astype(F32)
-    for z in range(wide_ref.shape[1]):
-        for x in range(NX):
-            at = (z * NX + x) * OWN
-            wide_ref[x, z] = block[at : at + OWN]
+def widen(term_ref, wide_ref, narrow, wide, arrived, left):
+    bands = narrow.shape[0]
+    per = NZ // bands
+    size = per * NX * OWN
+    reads = [pltpu.make_async_copy(term_ref.at[pl.ds(i * size, size)], narrow.at[i], arrived.at[i]) for i in range(bands)]
+    writes = [pltpu.make_async_copy(wide.at[i], wide_ref.at[:, pl.ds(i * per, per)], left.at[i]) for i in range(bands)]
+    for copy in reads:
+        copy.start()
+    for i in range(bands):
+        reads[i].wait()
+        block = narrow[i].astype(F32)
+        for z in range(per):
+            for x in range(NX):
+                at = (z * NX + x) * OWN
+                wide[i, x, z] = block[at : at + OWN]
+        writes[i].start()
+    for copy in writes:
+        copy.wait()
 
 
 def left_terms(term_ref, error_ref, q_ref, left_ref, parts):
@@ -205,12 +217,19 @@
     core = lax.axis_index("core")
     place = jnp.stack([lax.axis_index("z") * NX + lax.axis_index("x"), core]).astype(jnp.int32)
 
+    bands = NZ // 2
+    anywhere = pl.BlockSpec(memory_space=pl.ANY)
     wide = pl.pallas_call(
         widen,
         out_shape=array(NX, NZ, OWN, width),
-        grid=(NZ // 2,),
-        in_specs=[pl.BlockSpec((2 * NX * OWN, width), lambda i: (i, 0))],
-        out_specs=pl.BlockSpec((NX, 2, OWN, width), lambda i: (0, i, 0, 0)),
+        in_specs=[anywhere],
+        out_specs=anywhere,
+        scratch_shapes=[
+            pltpu.VMEM((bands, rows // bands, width), BF16),
+            pltpu.VMEM((bands, NX, NZ // bands, OWN, width), F32),
+            pltpu.SemaphoreType.DMA((bands,)),
+            pltpu.SemaphoreType.DMA((bands,)),
+        ],
         compiler_params=pltpu.CompilerParams(vmem_limit_bytes=60 * MIB),
     )(term)
     left = pl.pallas_call(
@@ -254,7 +273,6 @@
     )(left, left_own)
 
     summed = scatter(wide.reshape(rows, width), "x")
-    anywhere = pl.BlockSpec(memory_space=pl.ANY)
     summed = pl.pallas_call(
         hand_on,
         out_shape=array(*summed.shape),

time: 170 us -> 168 us (0.988)
  Pallas kernels: 22.5 us -> 20.6 us
    pallas_call x1, Pallas kernels: 5.77 us -> 3.85 us  [on_device(): pl.pallas_call(widen, out_shape=array(NX, NZ, OWN, width), in_specs=[anyw...]
where the time goes in v6:
time: 168 us; the launch traced here: 167 us
  blocking collectives  63 us (38%)
  waiting for transfers between devices  46.9 us (28%)
  Pallas kernels  20.6 us (12%)
  starting transfers between devices  18 us (11%)
  between operations  14.2 us (8%)
  other arithmetic  2.64 us (2%)
    all_to_all x3, blocking collectives, exchange(): return lax.all_to_all(value, axes, 0, 0, tiled=True)  63 us
    all_to_all x3, waiting for transfers between devices, exchange(): return lax.all_to_all(value, axes, 0, 0, tiled=True)  35.6 us
    all_to_all x3, starting transfers between devices, exchange(): return lax.all_to_all(value, axes, 0, 0, tiled=True)  14.1 us
    reduce_scatter x2, waiting for transfers between devices, scatter(): return lax.psum_scatter(value, axis, scatter_dimension=0, tiled=True)  6.89 us
    pallas_call x1, Pallas kernels, on_device(): pl.pallas_call(triangle, out_shape=(array(RANK, RANK), array(OWN, RANK)),...  6.6 us
    pallas_call x1, Pallas kernels, on_device(): pl.pallas_call(left_terms, out_shape=array(half, LANES), grid=(2,), in_sp...  4.89 us
    pallas_call x1, Pallas kernels, on_device(): pl.pallas_call(widen, out_shape=array(NX, NZ, OWN, width), in_specs=[anyw...  3.85 us
    ppermute x2, starting transfers between devices, swap(): return lax.ppermute(value, 'core', [(i, NC - 1 - i) for i in range(NC)])  3.84 us
  transfers between devices with their start and end apart: 7, of which 6 were waited for; matrix products, arithmetic and copies ran while one was open for 2% of the time, Pallas kernels for 10%

profile of v6, /device:TPU:6, one launch (start us, length us, event | category | flops | bytes accessed | tf_op | source)
XLA Modules:
  0.0 166.9 jit_solution(14944766246493984752)
XLA Ops:
  7.2 0.0 reduce-scatter.3.cloned.1.call-start
  7.2 3.9 %shard_map.72 = f32[4,12,8,4096]{3,2,1,0:T(8,128)} custom-call(bf16[384,4096]{1,0:T(8,128)(2,1)} %bitcast.14), custom_call_target="tpu_custom_call" | custom-call | tf_op jit(solution)/shard_map/pallas_call | solution.py:222
  11.1 0.0 reduce-scatter.3.cloned.1.call-update
  11.1 0.0 copy-start
  11.1 0.0 copy-start.1
  11.1 4.9 %shard_map.67 = f32[192,128]{1,0:T(8,128)} custom-call(bf16[384,4096]{1,0:T(8,128)(2,1)} %bitcast.15, f32[8,4096]{1,0:T(8,128)} %bitcast.18, f32[64,4096]{1,0:T(8,128)} %bitcast.23), custom_call_target="tpu_custom_call" | custom-call | tf_op jit(solution)/shard_map/pallas_call | solution.py:235
  16.0 26.9 %all_to_all.30 = f32[24,8,128]{2,1,0:T(8,128)S(1)} all-to-all(f32[24,8,128]{2,1,0:T(8,128)} %bitcast.24), channel_id=1, replica_groups=mesh['y'=8,'core'=2,'z'=12,'x'=4] {'z','core'}, dimensions={0} | all-to-all | bytes 196608 | tf_op jit(solution)/shard_map/all_to_all | solution.py:35
  43.0 19.0 %all_to_all.31 = f32[32,8,128]{2,1,0:T(8,128)S(1)} all-to-all(f32[32,8,128]{2,1,0:T(8,128)S(1)} %broadcast_in_dim.10), channel_id=1, replica_groups=mesh['y'=8,'core'=2,'z'=12,'x'=4] {'y','x'}, dimensions={0} | all-to-all | bytes 262144 | tf_op jit(solution)/shard_map/all_to_all | solution.py:35
  62.0 0.7 broadcast_in_dim.11
  62.6 3.8 %all-to-all-start.2 = ((f32[24,8,128]{2,1,0:T(8,128)}), f32[24,8,128]{2,1,0:T(8,128)S(1)}, u32[]{:S(2)}, u32[]{:S(2)}) async-start(f32[24,8,128]{2,1,0:T(8,128)} %broadcast_in_dim.11), calls=%async_computation.2 | async-start | bytes 196608 | tf_op jit(solution)/shard_map/all_to_all | solution.py:35
  66.5 0.1 pad_add_fusion.s_ref
  66.5 11.4 %all-to-all-done.2 = f32[24,8,128]{2,1,0:T(8,128)S(1)} async-done(((f32[24,8,128]{2,1,0:T(8,128)}), f32[24,8,128]{2,1,0:T(8,128)S(1)}, u32[]{:S(2)}, u32[]{:S(2)}) %all-to-all-start.2) | async-done | bytes 98336 | tf_op jit(solution)/shard_map/all_to_all | solution.py:35
  77.9 0.0 copy-done
  77.9 0.0 copy-done.1
  77.9 2.7 %shard_map.68 = (f32[8,64,256]{2,1,0:T(8,128)S(1)}, f32[8,64,256]{2,1,0:T(8,128)S(1)}, f32[8,64]{1,0:T(8,128)S(1)}) custom-call(s32[2]{0:T(128)S(1)} %pad_add_fusion.s_ref, f32[192,128]{1,0:T(8,128)S(1)} %bitcast.20, bf16[384,4096]{1,0:T(8,128)(2,1)S(1)} %bitcast.16, f32[8,4096]{1,0:T(8,128)S(1)} %bitcast.19), custom_call_target="tpu_custom_call" | custom-call | tf_op jit(solution)/shard_map/pallas_call | solution.py:249
  80.6 1.9 %collective-permute-start = (f32[8,64,256]{2,1,0:T(8,128)S(1)}, f32[8,64,256]{2,1,0:T(8,128)S(1)}, u32[]{:S(2)}, u32[]{:S(2)}) collective-permute-start(f32[8,64,256]{2,1,0:T(8,128)S(1)} %get-tuple-element.12), channel_id=1, source_target_pairs={{0,48},{48,0},{1,49},{49,1},{2,50},{50,2},{3,51},{51,3},{4,52},{52... | collective-permute-start | bytes 1572872 | tf_op jit(solution)/shard_map/ppermute | solution.py:47
  82.6 1.9 %collective-permute-done = f32[8,64,256]{2,1,0:T(8,128)S(1)} collective-permute-done((f32[8,64,256]{2,1,0:T(8,128)S(1)}, f32[8,64,256]{2,1,0:T(8,128)S(1)}, u32[]{:S(2)}, u32[]{:S(2)}) %collective-permute-start) | collective-permute-done | bytes 524320 | tf_op jit(solution)/shard_map/ppermute | solution.py:47
  84.5 0.9 add.14._
  85.3 5.3 %all-to-all-start.3 = ((f32[32,16,256]{2,1,0:T(8,128)}), f32[32,16,256]{2,1,0:T(8,128)S(1)}, u32[]{:S(2)}, u32[]{:S(2)}) async-start(f32[32,16,256]{2,1,0:T(8,128)} %bitcast.7), calls=%async_computation.3 | async-start | bytes 1048576 | tf_op jit(solution)/shard_map/all_to_all | solution.py:35
  90.7 0.0 reduce-scatter.5.cloned.1.call-start
  90.7 0.0 reduce-scatter.3.cloned.1.call-done.__
  90.7 0.7 reduce-scatter.5.cloned.1.call-update
  91.4 16.7 %all-to-all-done.3 = f32[32,16,256]{2,1,0:T(8,128)S(1)} async-done(((f32[32,16,256]{2,1,0:T(8,128)}), f32[32,16,256]{2,1,0:T(8,128)S(1)}, u32[]{:S(2)}, u32[]{:S(2)}) %all-to-all-start.3) | async-done | bytes 524320 | tf_op jit(solution)/shard_map/all_to_all | solution.py:35
  108.2 17.1 %all_to_all.32 = f32[12,16,256]{2,1,0:T(8,128)S(1)} all-to-all(f32[12,16,256]{2,1,0:T(8,128)S(1)} %broadcast_in_dim.12), channel_id=1, replica_groups=mesh['y'=8,'core'=2,'z'=12,'x'=4] {'z'}, dimensions={0} | all-to-all | bytes 393216 | tf_op jit(solution)/shard_map/all_to_all | solution.py:35
  125.3 0.9 broadcast_in_dim.13
  126.2 5.0 %all-to-all-start.5 = ((f32[32,16,256]{2,1,0:T(8,128)}), f32[32,16,256]{2,1,0:T(8,128)S(1)}, u32[]{:S(2)}, u32[]{:S(2)}) async-start(f32[32,16,256]{2,1,0:T(8,128)} %broadcast_in_dim.13), calls=%async_computation.5 | async-start | bytes 1048576 | tf_op jit(solution)/shard_map/all_to_all | solution.py:35
  131.2 0.0 copy-start.2
  131.2 6.6 %shard_map.69 = (f32[64,64]{1,0:T(8,128)S(1)}, f32[8,64]{1,0:T(8,128)S(1)}) custom-call(f32[192,128]{1,0:T(8,128)S(1)} %bitcast.21, f32[8,64]{1,0:T(8,128)S(1)} %get-tuple-element.13.own_ref), custom_call_target="tpu_custom_call" | custom-call | flops 20000000000 | bytes 98304 | tf_op jit(solution)/shard_map/pallas_call | solution.py:268
  137.8 7.4 %all-to-all-done.5 = f32[32,16,256]{2,1,0:T(8,128)S(1)} async-done(((f32[32,16,256]{2,1,0:T(8,128)}), f32[32,16,256]{2,1,0:T(8,128)S(1)}, u32[]{:S(2)}, u32[]{:S(2)}) %all-to-all-start.5) | async-done | bytes 524320 | tf_op jit(solution)/shard_map/all_to_all | solution.py:35
  145.2 0.4 shard_map.70.mine_ref
  145.7 1.9 %collective-permute-start.1 = (f32[8,64,256]{2,1,0:T(8,128)S(1)}, f32[8,64,256]{2,1,0:T(8,128)S(1)}, u32[]{:S(2)}, u32[]{:S(2)}) collective-permute-start(f32[8,64,256]{2,1,0:T(8,128)S(1)} %shard_map.70.mine_ref), channel_id=1, source_target_pairs={{0,48},{48,0},{1,49},{49,1},{2,50},{50,2},{3,51},{51,3},{4,52},{52... | collective-permute-start | bytes 1572872 | tf_op jit(solution)/shard_map/ppermute | solution.py:47
  147.6 1.9 %collective-permute-done.1.other_ref = f32[8,64,256]{2,1,0:T(8,128)S(1)} collective-permute-done((f32[8,64,256]{2,1,0:T(8,128)S(1)}, f32[8,64,256]{2,1,0:T(8,128)S(1)}, u32[]{:S(2)}, u32[]{:S(2)}) %collective-permute-start.1) | collective-permute-done | bytes 524320 | tf_op jit(solution)/shard_map/ppermute | solution.py:47
  149.5 0.0 copy-done.2
  149.5 2.1 %shard_map.71 = (f32[64,4096]{1,0:T(8,128)}, f32[8,4096]{1,0:T(8,128)S(1)}, f32[8,4096]{1,0:T(8,128)}) custom-call(s32[2]{0:T(128)S(1)} %pad_add_fusion.s_ref, f32[8,64,256]{2,1,0:T(8,128)S(1)} %shard_map.70.mine_ref, f32[8,64,256]{2,1,0:T(8,128)S(1)} %collective-permute-done.1.other_ref, f32[8,64]{1,0:T(8,128)S(1)} %get-tuple-element.15.left_ref, ...), custom_call_target="tpu_custom_call" | custom-call | tf_op jit(solution)/shard_map/pallas_call | solution.py:295
  151.6 6.9 %reduce-scatter.5.cloned.1.call-done = f32[8,4096]{1,0:T(8,128)} async-done(((f32[96,4096]{1,0:T(8,128)}), f32[8,4096]{1,0:T(8,128)}) %reduce-scatter.5.cloned.1.call-update) | async-done | bytes 131088 | tf_op jit(solution)/shard_map/reduce_scatter | solution.py:43
  158.5 1.6 subtract_bitcast_fusion
  (7 shorter events, 0.2 us)
Async XLA Ops:
  7.2 83.6 %reduce-scatter.3.cloned.1.call-start = ((), (), s32[]{:S(2)}) async-start(), calls=%async_computation.8 | async-start | bytes 7864320 | tf_op jit(solution)/shard_map/reduce_scatter | solution.py:43
  11.1 66.8 %copy-start = (bf16[1,1,384,4096]{3,2,1,0:T(8,128)(2,1)S(1)}, bf16[1,1,384,4096]{3,2,1,0:T(8,128)(2,1)}, u32[]{:S(2)}) copy-start(bf16[1,1,384,4096]{3,2,1,0:T(8,128)(2,1)} %param.4) | copy-start | bytes 9437188
  11.1 66.8 %copy-start.1 = (f32[1,8,4096]{2,1,0:T(8,128)S(1)}, f32[1,8,4096]{2,1,0:T(8,128)}, u32[]{:S(2)}) copy-start(f32[1,8,4096]{2,1,0:T(8,128)} %param.5) | copy-start | bytes 393220
  62.6 15.3 %all-to-all-start.2 = ((f32[24,8,128]{2,1,0:T(8,128)}), f32[24,8,128]{2,1,0:T(8,128)S(1)}, u32[]{:S(2)}, u32[]{:S(2)}) async-start(f32[24,8,128]{2,1,0:T(8,128)} %broadcast_in_dim.11), calls=%async_computation.2 | async-start | bytes 196608 | tf_op jit(solution)/shard_map/all_to_all | solution.py:35
  80.6 3.8 %collective-permute-start = (f32[8,64,256]{2,1,0:T(8,128)S(1)}, f32[8,64,256]{2,1,0:T(8,128)S(1)}, u32[]{:S(2)}, u32[]{:S(2)}) collective-permute-start(f32[8,64,256]{2,1,0:T(8,128)S(1)} %get-tuple-element.12), channel_id=1, source_target_pairs={{0,48},{48,0},{1,49},{49,1},{2,50},{50,2},{3,51},{51,3},{4,52},{52... | collective-permute-start | bytes 1572872 | tf_op jit(solution)/shard_map/ppermute | solution.py:47
  85.3 22.8 %all-to-all-start.3 = ((f32[32,16,256]{2,1,0:T(8,128)}), f32[32,16,256]{2,1,0:T(8,128)S(1)}, u32[]{:S(2)}, u32[]{:S(2)}) async-start(f32[32,16,256]{2,1,0:T(8,128)} %bitcast.7), calls=%async_computation.3 | async-start | bytes 1048576 | tf_op jit(solution)/shard_map/all_to_all | solution.py:35
  90.7 67.8 %reduce-scatter.5.cloned.1.call-start = ((), (), s32[]{:S(2)}) async-start(), calls=%async_computation.9 | async-start | bytes 1703936 | tf_op jit(solution)/shard_map/reduce_scatter | solution.py:43
  126.2 19.0 %all-to-all-start.5 = ((f32[32,16,256]{2,1,0:T(8,128)}), f32[32,16,256]{2,1,0:T(8,128)S(1)}, u32[]{:S(2)}, u32[]{:S(2)}) async-start(f32[32,16,256]{2,1,0:T(8,128)} %broadcast_in_dim.13), calls=%async_computation.5 | async-start | bytes 1048576 | tf_op jit(solution)/shard_map/all_to_all | solution.py:35
  131.2 18.3 %copy-start.2 = (f32[8,4096]{1,0:T(8,128)S(1)}, f32[8,4096]{1,0:T(8,128)}, u32[]{:S(2)}) copy-start(f32[8,4096]{1,0:T(8,128)} %weight_ref.1) | copy-start | bytes 393220
  145.7 3.8 %collective-permute-start.1 = (f32[8,64,256]{2,1,0:T(8,128)S(1)}, f32[8,64,256]{2,1,0:T(8,128)S(1)}, u32[]{:S(2)}, u32[]{:S(2)}) collective-permute-start(f32[8,64,256]{2,1,0:T(8,128)S(1)} %shard_map.70.mine_ref), channel_id=1, source_target_pairs={{0,48},{48,0},{1,49},{49,1},{2,50},{50,2},{3,51},{51,3},{4,52},{52... | collective-permute-start | bytes 1572872 | tf_op jit(solution)/shard_map/ppermute | solution.py:47
Sparse Core Ops, SparseCore 0:
  11.2 78.2 reduce-scatter.2
  94.6 63.8 reduce-scatter.4

commit v7 on v6

--- a/solution.py
+++ b/solution.py
@@ -177,7 +177,7 @@
         q_ref[k] = products(inverse_ref[...], blocks_ref[k])
 
 
-def finish(s_ref, mine_ref, other_ref, left_ref, weight_ref, q_ref, approx_out, weight_out):
+def finish(s_ref, mine_ref, other_ref, left_ref, error_ref, weight_ref, q_ref, change_out, weight_out):
     step = pl.program_id(0)
     cols = mine_ref.shape[2]
 
@@ -187,7 +187,7 @@
             block = blocks_ref[k]
             q_ref[:, at] = block
             approx = products(left_ref[...], block)
-            approx_out[:, at] = approx
+            change_out[:, at] = error_ref[:, at] - approx
             weight_out[:, at] = weight_ref[:, at] - 0.5 * approx
 
     pl.when(step == s_ref[1])(functools.partial(run, mine_ref))
@@ -217,7 +217,7 @@
     core = lax.axis_index("core")
     place = jnp.stack([lax.axis_index("z") * NX + lax.axis_index("x"), core]).astype(jnp.int32)
 
-    bands = NZ // 2
+    bands = NZ
     anywhere = pl.BlockSpec(memory_space=pl.ANY)
     wide = pl.pallas_call(
         widen,
@@ -292,15 +292,15 @@
     )(gathered(block, ("y", "x"), NY * NX).reshape(NY, RANK, cols), inverse)
     other = swap(mine)
     side = pl.BlockSpec((OWN, width // 2), lambda i, _: (0, i))
-    q_turned, approx, weight_next = call(
+    q_turned, change, weight_next = call(
         finish,
         16,
         (2,),
-        [whole((NY, RANK, cols)), whole((NY, RANK, cols)), whole((OWN, RANK)), side],
+        [whole((NY, RANK, cols)), whole((NY, RANK, cols)), whole((OWN, RANK)), side, side],
         [pl.BlockSpec((RANK, width // 2), lambda i, _: (0, i)), side, side],
         [array(RANK, width), array(OWN, width), array(OWN, width)],
-    )(place, mine, other, left_hat, weight)
-    return (q_turned.T, (summed + error - approx)[None], weight_next)
+    )(place, mine, other, left_hat, error, weight)
+    return (q_turned.T, (summed + change)[None], weight_next)
 
 
 def solution(mesh):

time: 168 us -> 168 us (level)
  no operation moved by 1% of the time
where the time goes in v7:
time: 168 us; the launch traced here: 167 us
  blocking collectives  63 us (38%)
  waiting for transfers between devices  47.1 us (28%)
  Pallas kernels  20.6 us (12%)
  starting transfers between devices  18.1 us (11%)
  between operations  14.2 us (8%)
  other arithmetic  2.64 us (2%)
    all_to_all x3, blocking collectives, exchange(): return lax.all_to_all(value, axes, 0, 0, tiled=True)  63 us
    all_to_all x3, waiting for transfers between devices, exchange(): return lax.all_to_all(value, axes, 0, 0, tiled=True)  35.5 us
    all_to_all x3, starting transfers between devices, exchange(): return lax.all_to_all(value, axes, 0, 0, tiled=True)  14.2 us
    reduce_scatter x2, waiting for transfers between devices, scatter(): return lax.psum_scatter(value, axis, scatter_dimension=0, tiled=True)  7.12 us
    pallas_call x1, Pallas kernels, on_device(): pl.pallas_call(triangle, out_shape=(array(RANK, RANK), array(OWN, RANK)),...  6.6 us
    pallas_call x1, Pallas kernels, on_device(): pl.pallas_call(left_terms, out_shape=array(half, LANES), grid=(2,), in_sp...  4.89 us
    ppermute x2, starting transfers between devices, swap(): return lax.ppermute(value, 'core', [(i, NC - 1 - i) for i in range(NC)])  3.84 us
    pallas_call x1, Pallas kernels, on_device(): pl.pallas_call(widen, out_shape=array(NX, NZ, OWN, width), in_specs=[anyw...  3.83 us
  transfers between devices with their start and end apart: 7, of which 6 were waited for; matrix products, arithmetic and copies ran while one was open for 2% of the time, Pallas kernels for 10%

profile of v7, /device:TPU:6, one launch (start us, length us, event | category | flops | bytes accessed | tf_op | source)
XLA Modules:
  0.0 167.1 jit_solution(11485308521975501805)
XLA Ops:
  7.2 0.0 reduce-scatter.3.cloned.1.call-start
  7.2 3.8 %shard_map.72 = f32[4,12,8,4096]{3,2,1,0:T(8,128)} custom-call(bf16[384,4096]{1,0:T(8,128)(2,1)} %bitcast.13), custom_call_target="tpu_custom_call" | custom-call | tf_op jit(solution)/shard_map/pallas_call | solution.py:222
  11.0 0.0 reduce-scatter.3.cloned.1.call-update
  11.1 0.0 copy-start
  11.1 0.0 copy-start.1
  11.1 4.9 %shard_map.67 = f32[192,128]{1,0:T(8,128)} custom-call(bf16[384,4096]{1,0:T(8,128)(2,1)} %bitcast.14, f32[8,4096]{1,0:T(8,128)} %bitcast.17, f32[64,4096]{1,0:T(8,128)} %bitcast.23), custom_call_target="tpu_custom_call" | custom-call | tf_op jit(solution)/shard_map/pallas_call | solution.py:235
  16.0 26.9 %all_to_all.30 = f32[24,8,128]{2,1,0:T(8,128)S(1)} all-to-all(f32[24,8,128]{2,1,0:T(8,128)} %bitcast.24), channel_id=1, replica_groups=mesh['y'=8,'core'=2,'z'=12,'x'=4] {'z','core'}, dimensions={0} | all-to-all | bytes 196608 | tf_op jit(solution)/shard_map/all_to_all | solution.py:35
  42.9 19.0 %all_to_all.31 = f32[32,8,128]{2,1,0:T(8,128)S(1)} all-to-all(f32[32,8,128]{2,1,0:T(8,128)S(1)} %broadcast_in_dim.10), channel_id=1, replica_groups=mesh['y'=8,'core'=2,'z'=12,'x'=4] {'y','x'}, dimensions={0} | all-to-all | bytes 262144 | tf_op jit(solution)/shard_map/all_to_all | solution.py:35
  61.9 0.7 broadcast_in_dim.11
  62.6 3.8 %all-to-all-start.2 = ((f32[24,8,128]{2,1,0:T(8,128)}), f32[24,8,128]{2,1,0:T(8,128)S(1)}, u32[]{:S(2)}, u32[]{:S(2)}) async-start(f32[24,8,128]{2,1,0:T(8,128)} %broadcast_in_dim.11), calls=%async_computation.2 | async-start | bytes 196608 | tf_op jit(solution)/shard_map/all_to_all | solution.py:35
  66.4 0.1 pad_add_fusion.s_ref
  66.5 11.4 %all-to-all-done.2 = f32[24,8,128]{2,1,0:T(8,128)S(1)} async-done(((f32[24,8,128]{2,1,0:T(8,128)}), f32[24,8,128]{2,1,0:T(8,128)S(1)}, u32[]{:S(2)}, u32[]{:S(2)}) %all-to-all-start.2) | async-done | bytes 98336 | tf_op jit(solution)/shard_map/all_to_all | solution.py:35
  77.9 0.0 copy-done
  77.9 0.0 copy-done.1
  77.9 2.7 %shard_map.68 = (f32[8,64,256]{2,1,0:T(8,128)S(1)}, f32[8,64,256]{2,1,0:T(8,128)S(1)}, f32[8,64]{1,0:T(8,128)S(1)}) custom-call(s32[2]{0:T(128)S(1)} %pad_add_fusion.s_ref, f32[192,128]{1,0:T(8,128)S(1)} %bitcast.20, bf16[384,4096]{1,0:T(8,128)(2,1)S(1)} %bitcast.15, f32[8,4096]{1,0:T(8,128)S(1)} %bitcast.18), custom_call_target="tpu_custom_call" | custom-call | tf_op jit(solution)/shard_map/pallas_call | solution.py:249
  80.6 1.9 %collective-permute-start = (f32[8,64,256]{2,1,0:T(8,128)S(1)}, f32[8,64,256]{2,1,0:T(8,128)S(1)}, u32[]{:S(2)}, u32[]{:S(2)}) collective-permute-start(f32[8,64,256]{2,1,0:T(8,128)S(1)} %get-tuple-element.12), channel_id=1, source_target_pairs={{0,48},{48,0},{1,49},{49,1},{2,50},{50,2},{3,51},{51,3},{4,52},{52... | collective-permute-start | bytes 1572872 | tf_op jit(solution)/shard_map/ppermute | solution.py:47
  82.6 1.9 %collective-permute-done = f32[8,64,256]{2,1,0:T(8,128)S(1)} collective-permute-done((f32[8,64,256]{2,1,0:T(8,128)S(1)}, f32[8,64,256]{2,1,0:T(8,128)S(1)}, u32[]{:S(2)}, u32[]{:S(2)}) %collective-permute-start) | collective-permute-done | bytes 524320 | tf_op jit(solution)/shard_map/ppermute | solution.py:47
  84.4 0.9 add.14._
  85.3 5.3 %all-to-all-start.3 = ((f32[32,16,256]{2,1,0:T(8,128)}), f32[32,16,256]{2,1,0:T(8,128)S(1)}, u32[]{:S(2)}, u32[]{:S(2)}) async-start(f32[32,16,256]{2,1,0:T(8,128)} %bitcast.7), calls=%async_computation.3 | async-start | bytes 1048576 | tf_op jit(solution)/shard_map/all_to_all | solution.py:35
  90.6 0.0 reduce-scatter.5.cloned.1.call-start
  90.7 0.0 reduce-scatter.3.cloned.1.call-done.__
  90.7 0.7 reduce-scatter.5.cloned.1.call-update
  91.4 16.7 %all-to-all-done.3 = f32[32,16,256]{2,1,0:T(8,128)S(1)} async-done(((f32[32,16,256]{2,1,0:T(8,128)}), f32[32,16,256]{2,1,0:T(8,128)S(1)}, u32[]{:S(2)}, u32[]{:S(2)}) %all-to-all-start.3) | async-done | bytes 524320 | tf_op jit(solution)/shard_map/all_to_all | solution.py:35
  108.2 17.1 %all_to_all.32 = f32[12,16,256]{2,1,0:T(8,128)S(1)} all-to-all(f32[12,16,256]{2,1,0:T(8,128)S(1)} %broadcast_in_dim.12), channel_id=1, replica_groups=mesh['y'=8,'core'=2,'z'=12,'x'=4] {'z'}, dimensions={0} | all-to-all | bytes 393216 | tf_op jit(solution)/shard_map/all_to_all | solution.py:35
  125.3 0.9 broadcast_in_dim.13
  126.2 5.1 %all-to-all-start.5 = ((f32[32,16,256]{2,1,0:T(8,128)}), f32[32,16,256]{2,1,0:T(8,128)S(1)}, u32[]{:S(2)}, u32[]{:S(2)}) async-start(f32[32,16,256]{2,1,0:T(8,128)} %broadcast_in_dim.13), calls=%async_computation.5 | async-start | bytes 1048576 | tf_op jit(solution)/shard_map/all_to_all | solution.py:35
  131.2 0.0 copy-start.2
  131.2 6.6 %shard_map.69 = (f32[64,64]{1,0:T(8,128)S(1)}, f32[8,64]{1,0:T(8,128)S(1)}) custom-call(f32[192,128]{1,0:T(8,128)S(1)} %bitcast.21, f32[8,64]{1,0:T(8,128)S(1)} %get-tuple-element.13.own_ref), custom_call_target="tpu_custom_call" | custom-call | flops 20000000000 | bytes 98304 | tf_op jit(solution)/shard_map/pallas_call | solution.py:268
  137.8 7.4 %all-to-all-done.5 = f32[32,16,256]{2,1,0:T(8,128)S(1)} async-done(((f32[32,16,256]{2,1,0:T(8,128)}), f32[32,16,256]{2,1,0:T(8,128)S(1)}, u32[]{:S(2)}, u32[]{:S(2)}) %all-to-all-start.5) | async-done | bytes 524320 | tf_op jit(solution)/shard_map/all_to_all | solution.py:35
  145.2 0.4 shard_map.70.mine_ref
  145.7 1.9 %collective-permute-start.1 = (f32[8,64,256]{2,1,0:T(8,128)S(1)}, f32[8,64,256]{2,1,0:T(8,128)S(1)}, u32[]{:S(2)}, u32[]{:S(2)}) collective-permute-start(f32[8,64,256]{2,1,0:T(8,128)S(1)} %shard_map.70.mine_ref), channel_id=1, source_target_pairs={{0,48},{48,0},{1,49},{49,1},{2,50},{50,2},{3,51},{51,3},{4,52},{52... | collective-permute-start | bytes 1572872 | tf_op jit(solution)/shard_map/ppermute | solution.py:47
  147.6 1.9 %collective-permute-done.1.other_ref = f32[8,64,256]{2,1,0:T(8,128)S(1)} collective-permute-done((f32[8,64,256]{2,1,0:T(8,128)S(1)}, f32[8,64,256]{2,1,0:T(8,128)S(1)}, u32[]{:S(2)}, u32[]{:S(2)}) %collective-permute-start.1) | collective-permute-done | bytes 524320 | tf_op jit(solution)/shard_map/ppermute | solution.py:47
  149.5 0.0 copy-done.2
  149.5 2.1 %shard_map.71 = (f32[64,4096]{1,0:T(8,128)}, f32[8,4096]{1,0:T(8,128)S(1)}, f32[8,4096]{1,0:T(8,128)}) custom-call(s32[2]{0:T(128)S(1)} %pad_add_fusion.s_ref, f32[8,64,256]{2,1,0:T(8,128)S(1)} %shard_map.70.mine_ref, f32[8,64,256]{2,1,0:T(8,128)S(1)} %collective-permute-done.1.other_ref, f32[8,64]{1,0:T(8,128)S(1)} %get-tuple-element.15.left_ref, ...), custom_call_target="tpu_custom_call" | custom-call | tf_op jit(solution)/shard_map/pallas_call | solution.py:295
  151.6 7.1 %reduce-scatter.5.cloned.1.call-done = f32[8,4096]{1,0:T(8,128)} async-done(((f32[96,4096]{1,0:T(8,128)}), f32[8,4096]{1,0:T(8,128)}) %reduce-scatter.5.cloned.1.call-update) | async-done | bytes 131088 | tf_op jit(solution)/shard_map/reduce_scatter | solution.py:43
  158.7 1.6 add_bitcast_fusion
  (7 shorter events, 0.2 us)
Async XLA Ops:
  7.2 83.5 %reduce-scatter.3.cloned.1.call-start = ((), (), s32[]{:S(2)}) async-start(), calls=%async_computation.8 | async-start | bytes 7864320 | tf_op jit(solution)/shard_map/reduce_scatter | solution.py:43
  11.1 66.8 %copy-start = (bf16[1,1,384,4096]{3,2,1,0:T(8,128)(2,1)S(1)}, bf16[1,1,384,4096]{3,2,1,0:T(8,128)(2,1)}, u32[]{:S(2)}) copy-start(bf16[1,1,384,4096]{3,2,1,0:T(8,128)(2,1)} %param.4) | copy-start | bytes 9437188
  11.1 66.8 %copy-start.1 = (f32[1,8,4096]{2,1,0:T(8,128)S(1)}, f32[1,8,4096]{2,1,0:T(8,128)}, u32[]{:S(2)}) copy-start(f32[1,8,4096]{2,1,0:T(8,128)} %param.5) | copy-start | bytes 393220
  62.6 15.3 %all-to-all-start.2 = ((f32[24,8,128]{2,1,0:T(8,128)}), f32[24,8,128]{2,1,0:T(8,128)S(1)}, u32[]{:S(2)}, u32[]{:S(2)}) async-start(f32[24,8,128]{2,1,0:T(8,128)} %broadcast_in_dim.11), calls=%async_computation.2 | async-start | bytes 196608 | tf_op jit(solution)/shard_map/all_to_all | solution.py:35
  80.6 3.8 %collective-permute-start = (f32[8,64,256]{2,1,0:T(8,128)S(1)}, f32[8,64,256]{2,1,0:T(8,128)S(1)}, u32[]{:S(2)}, u32[]{:S(2)}) collective-permute-start(f32[8,64,256]{2,1,0:T(8,128)S(1)} %get-tuple-element.12), channel_id=1, source_target_pairs={{0,48},{48,0},{1,49},{49,1},{2,50},{50,2},{3,51},{51,3},{4,52},{52... | collective-permute-start | bytes 1572872 | tf_op jit(solution)/shard_map/ppermute | solution.py:47
  85.3 22.8 %all-to-all-start.3 = ((f32[32,16,256]{2,1,0:T(8,128)}), f32[32,16,256]{2,1,0:T(8,128)S(1)}, u32[]{:S(2)}, u32[]{:S(2)}) async-start(f32[32,16,256]{2,1,0:T(8,128)} %bitcast.7), calls=%async_computation.3 | async-start | bytes 1048576 | tf_op jit(solution)/shard_map/all_to_all | solution.py:35
  90.6 68.1 %reduce-scatter.5.cloned.1.call-start = ((), (), s32[]{:S(2)}) async-start(), calls=%async_computation.9 | async-start | bytes 1703936 | tf_op jit(solution)/shard_map/reduce_scatter | solution.py:43
  126.2 19.0 %all-to-all-start.5 = ((f32[32,16,256]{2,1,0:T(8,128)}), f32[32,16,256]{2,1,0:T(8,128)S(1)}, u32[]{:S(2)}, u32[]{:S(2)}) async-start(f32[32,16,256]{2,1,0:T(8,128)} %broadcast_in_dim.13), calls=%async_computation.5 | async-start | bytes 1048576 | tf_op jit(solution)/shard_map/all_to_all | solution.py:35
  131.2 18.2 %copy-start.2 = (f32[8,4096]{1,0:T(8,128)S(1)}, f32[8,4096]{1,0:T(8,128)}, u32[]{:S(2)}) copy-start(f32[8,4096]{1,0:T(8,128)} %weight_ref.1) | copy-start | bytes 393220
  145.7 3.8 %collective-permute-start.1 = (f32[8,64,256]{2,1,0:T(8,128)S(1)}, f32[8,64,256]{2,1,0:T(8,128)S(1)}, u32[]{:S(2)}, u32[]{:S(2)}) collective-permute-start(f32[8,64,256]{2,1,0:T(8,128)S(1)} %shard_map.70.mine_ref), channel_id=1, source_target_pairs={{0,48},{48,0},{1,49},{49,1},{2,50},{50,2},{3,51},{51,3},{4,52},{52... | collective-permute-start | bytes 1572872 | tf_op jit(solution)/shard_map/ppermute | solution.py:47
Sparse Core Ops, SparseCore 0:
  11.2 78.2 reduce-scatter.2
  94.6 64.0 reduce-scatter.4

commit v8 on v7

--- a/solution.py
+++ b/solution.py
@@ -269,7 +269,7 @@
         triangle,
         out_shape=(array(RANK, RANK), array(OWN, RANK)),
         compiler_params=pltpu.CompilerParams(vmem_limit_bytes=8 * MIB),
-        cost_estimate=pl.CostEstimate(flops=20 * 10**9, bytes_accessed=4 * half * LANES, transcendentals=RANK),
+        cost_estimate=pl.CostEstimate(flops=4 * RANK**3, bytes_accessed=4 * half * LANES, transcendentals=RANK),
     )(left, left_own)
 
     summed = scatter(wide.reshape(rows, width), "x")

time: 168 us -> 181 us (1.077)
  blocking collectives: 63 us -> 98.4 us
  waiting for transfers between devices: 47.1 us -> 26.8 us
  starting transfers between devices: 18.1 us -> 14.3 us
    all_to_all x3 -> x4, blocking collectives: 63 us -> 98.4 us  [exchange(): return lax.all_to_all(value, axes, 0, 0, tiled=True)]
    all_to_all x3 -> x2, waiting for transfers between devices: 35.5 us -> 18.8 us  [exchange(): return lax.all_to_all(value, axes, 0, 0, tiled=True)]
    all_to_all x3 -> x2, starting transfers between devices: 14.2 us -> 10.3 us  [exchange(): return lax.all_to_all(value, axes, 0, 0, tiled=True)]
    reduce_scatter x2, waiting for transfers between devices: 7.12 us -> 4.16 us  [scatter(): return lax.psum_scatter(value, axis, scatter_dimension=0, tiled=True)]
  transfers between devices with their start and end apart: 7 -> 6, of which waited for: 6 -> 5; matrix products, arithmetic and copies ran while one was open for 2% -> 1% of each run, Pallas kernels for 10% -> 9%
where the time goes in v8:
time: 181 us; the launch traced here: 178 us
  blocking collectives  98.4 us (54%)
  waiting for transfers between devices  26.8 us (15%)
  Pallas kernels  20.6 us (11%)
  starting transfers between devices  14.3 us (8%)
  between operations  14.1 us (8%)
  other arithmetic  2.64 us (1%)
    all_to_all x4, blocking collectives, exchange(): return lax.all_to_all(value, axes, 0, 0, tiled=True)  98.4 us
    all_to_all x2, waiting for transfers between devices, exchange(): return lax.all_to_all(value, axes, 0, 0, tiled=True)  18.8 us
    all_to_all x2, starting transfers between devices, exchange(): return lax.all_to_all(value, axes, 0, 0, tiled=True)  10.3 us
    pallas_call x1, Pallas kernels, on_device(): pl.pallas_call(triangle, out_shape=(array(RANK, RANK), array(OWN, RANK)),...  6.6 us
    pallas_call x1, Pallas kernels, on_device(): pl.pallas_call(left_terms, out_shape=array(half, LANES), grid=(2,), in_sp...  4.89 us
    reduce_scatter x2, waiting for transfers between devices, scatter(): return lax.psum_scatter(value, axis, scatter_dimension=0, tiled=True)  4.16 us
    pallas_call x1, Pallas kernels, on_device(): pl.pallas_call(widen, out_shape=array(NX, NZ, OWN, width), in_specs=[anyw...  3.86 us
    ppermute x2, starting transfers between devices, swap(): return lax.ppermute(value, 'core', [(i, NC - 1 - i) for i in range(NC)])  3.84 us
  transfers between devices with their start and end apart: 6, of which 5 were waited for; matrix products, arithmetic and copies ran while one was open for 1% of the time, Pallas kernels for 9%

profile of v8, /device:TPU:6, one launch (start us, length us, event | category | flops | bytes accessed | tf_op | source)
XLA Modules:
  0.0 178.4 jit_solution(7688108559876094829)
XLA Ops:
  7.2 0.0 reduce-scatter.3.cloned.1.call-start
  7.2 3.9 %shard_map.72 = f32[4,12,8,4096]{3,2,1,0:T(8,128)} custom-call(bf16[384,4096]{1,0:T(8,128)(2,1)} %bitcast.13), custom_call_target="tpu_custom_call" | custom-call | tf_op jit(solution)/shard_map/pallas_call | solution.py:222
  11.1 0.0 reduce-scatter.3.cloned.1.call-update
  11.1 0.0 copy-start
  11.1 0.0 copy-start.1
  11.1 4.9 %shard_map.67 = f32[192,128]{1,0:T(8,128)} custom-call(bf16[384,4096]{1,0:T(8,128)(2,1)} %bitcast.14, f32[8,4096]{1,0:T(8,128)} %bitcast.17, f32[64,4096]{1,0:T(8,128)} %bitcast.24), custom_call_target="tpu_custom_call" | custom-call | tf_op jit(solution)/shard_map/pallas_call | solution.py:235
  16.0 26.9 %all_to_all.30 = f32[24,8,128]{2,1,0:T(8,128)S(1)} all-to-all(f32[24,8,128]{2,1,0:T(8,128)} %bitcast.25), channel_id=1, replica_groups=mesh['y'=8,'core'=2,'z'=12,'x'=4] {'z','core'}, dimensions={0} | all-to-all | bytes 196608 | tf_op jit(solution)/shard_map/all_to_all | solution.py:35
  43.0 19.0 %all_to_all.31 = f32[32,8,128]{2,1,0:T(8,128)S(1)} all-to-all(f32[32,8,128]{2,1,0:T(8,128)S(1)} %broadcast_in_dim.10), channel_id=1, replica_groups=mesh['y'=8,'core'=2,'z'=12,'x'=4] {'y','x'}, dimensions={0} | all-to-all | bytes 262144 | tf_op jit(solution)/shard_map/all_to_all | solution.py:35
  62.0 0.7 broadcast_in_dim.11
  62.6 3.8 %all-to-all-start.2 = ((f32[24,8,128]{2,1,0:T(8,128)}), f32[24,8,128]{2,1,0:T(8,128)S(1)}, u32[]{:S(2)}, u32[]{:S(2)}) async-start(f32[24,8,128]{2,1,0:T(8,128)} %broadcast_in_dim.11), calls=%async_computation.2 | async-start | bytes 196608 | tf_op jit(solution)/shard_map/all_to_all | solution.py:35
  66.5 0.0 reduce-scatter.5.cloned.1.call-start
  66.5 0.1 pad_add_fusion.s_ref
  66.6 11.4 %all-to-all-done.2 = f32[24,8,128]{2,1,0:T(8,128)S(1)} async-done(((f32[24,8,128]{2,1,0:T(8,128)}), f32[24,8,128]{2,1,0:T(8,128)S(1)}, u32[]{:S(2)}, u32[]{:S(2)}) %all-to-all-start.2) | async-done | bytes 98336 | tf_op jit(solution)/shard_map/all_to_all | solution.py:35
  77.9 0.0 copy-done
  78.0 0.0 copy-done.1
  78.0 2.7 %shard_map.68 = (f32[8,64,256]{2,1,0:T(8,128)S(1)}, f32[8,64,256]{2,1,0:T(8,128)S(1)}, f32[8,64]{1,0:T(8,128)S(1)}) custom-call(s32[2]{0:T(128)S(1)} %pad_add_fusion.s_ref, f32[192,128]{1,0:T(8,128)S(1)} %bitcast.20, bf16[384,4096]{1,0:T(8,128)(2,1)S(1)} %bitcast.15, f32[8,4096]{1,0:T(8,128)S(1)} %bitcast.18), custom_call_target="tpu_custom_call" | custom-call | tf_op jit(solution)/shard_map/pallas_call | solution.py:249
  80.7 1.9 %collective-permute-start = (f32[8,64,256]{2,1,0:T(8,128)S(1)}, f32[8,64,256]{2,1,0:T(8,128)S(1)}, u32[]{:S(2)}, u32[]{:S(2)}) collective-permute-start(f32[8,64,256]{2,1,0:T(8,128)S(1)} %get-tuple-element.12), channel_id=1, source_target_pairs={{0,48},{48,0},{1,49},{49,1},{2,50},{50,2},{3,51},{51,3},{4,52},{52... | collective-permute-start | bytes 1572872 | tf_op jit(solution)/shard_map/ppermute | solution.py:47
  82.6 1.9 %collective-permute-done = f32[8,64,256]{2,1,0:T(8,128)S(1)} collective-permute-done((f32[8,64,256]{2,1,0:T(8,128)S(1)}, f32[8,64,256]{2,1,0:T(8,128)S(1)}, u32[]{:S(2)}, u32[]{:S(2)}) %collective-permute-start) | collective-permute-done | bytes 524320 | tf_op jit(solution)/shard_map/ppermute | solution.py:47
  84.5 0.9 add.14._
  85.3 0.0 copy-start.3
  85.3 4.2 %reduce-scatter.3.cloned.1.call-done.__ = f32[96,4096]{1,0:T(8,128)} async-done(((f32[384,4096]{1,0:T(8,128)}), f32[96,4096]{1,0:T(8,128)}) %reduce-scatter.3.cloned.1.call-update) | async-done | bytes 1572880 | tf_op jit(solution)/shard_map/reduce_scatter | solution.py:43
  89.5 0.0 copy-start.2
  89.5 0.0 reduce-scatter.5.cloned.1.call-update
  89.5 0.0 copy-done.3
  89.5 27.0 %all_to_all.32 = f32[32,16,256]{2,1,0:T(8,128)S(1)} all-to-all(f32[32,16,256]{2,1,0:T(8,128)S(1)} %bitcast.23), channel_id=1, replica_groups=mesh['y'=8,'core'=2,'z'=12,'x'=4] {'y','x'}, dimensions={0} | all-to-all | bytes 1048576 | tf_op jit(solution)/shard_map/all_to_all | solution.py:35
  116.6 25.6 %all_to_all.33 = f32[12,16,256]{2,1,0:T(8,128)S(1)} all-to-all(f32[12,16,256]{2,1,0:T(8,128)S(1)} %broadcast_in_dim.12), channel_id=1, replica_groups=mesh['y'=8,'core'=2,'z'=12,'x'=4] {'z'}, dimensions={0} | all-to-all | bytes 393216 | tf_op jit(solution)/shard_map/all_to_all | solution.py:35
  142.2 0.9 broadcast_in_dim.13
  143.0 6.5 %all-to-all-start.5 = ((f32[32,16,256]{2,1,0:T(8,128)}), f32[32,16,256]{2,1,0:T(8,128)S(1)}, u32[]{:S(2)}, u32[]{:S(2)}) async-start(f32[32,16,256]{2,1,0:T(8,128)} %broadcast_in_dim.13), calls=%async_computation.5 | async-start | bytes 1048576 | tf_op jit(solution)/shard_map/all_to_all | solution.py:35
  149.6 6.6 %shard_map.69 = (f32[64,64]{1,0:T(8,128)S(1)}, f32[8,64]{1,0:T(8,128)S(1)}) custom-call(f32[192,128]{1,0:T(8,128)S(1)} %bitcast.21, f32[8,64]{1,0:T(8,128)S(1)} %get-tuple-element.13.own_ref), custom_call_target="tpu_custom_call" | custom-call | flops 1048576 | bytes 98304 | tf_op jit(solution)/shard_map/pallas_call | solution.py:268
  156.2 7.5 %all-to-all-done.5 = f32[32,16,256]{2,1,0:T(8,128)S(1)} async-done(((f32[32,16,256]{2,1,0:T(8,128)}), f32[32,16,256]{2,1,0:T(8,128)S(1)}, u32[]{:S(2)}, u32[]{:S(2)}) %all-to-all-start.5) | async-done | bytes 524320 | tf_op jit(solution)/shard_map/all_to_all | solution.py:35
  163.6 0.4 shard_map.70.mine_ref
  164.1 1.9 %collective-permute-start.1 = (f32[8,64,256]{2,1,0:T(8,128)S(1)}, f32[8,64,256]{2,1,0:T(8,128)S(1)}, u32[]{:S(2)}, u32[]{:S(2)}) collective-permute-start(f32[8,64,256]{2,1,0:T(8,128)S(1)} %shard_map.70.mine_ref), channel_id=1, source_target_pairs={{0,48},{48,0},{1,49},{49,1},{2,50},{50,2},{3,51},{51,3},{4,52},{52... | collective-permute-start | bytes 1572872 | tf_op jit(solution)/shard_map/ppermute | solution.py:47
  166.0 1.9 %collective-permute-done.1.other_ref = f32[8,64,256]{2,1,0:T(8,128)S(1)} collective-permute-done((f32[8,64,256]{2,1,0:T(8,128)S(1)}, f32[8,64,256]{2,1,0:T(8,128)S(1)}, u32[]{:S(2)}, u32[]{:S(2)}) %collective-permute-start.1) | collective-permute-done | bytes 524320 | tf_op jit(solution)/shard_map/ppermute | solution.py:47
  167.9 0.0 copy-done.2
  167.9 2.1 %shard_map.71 = (f32[64,4096]{1,0:T(8,128)}, f32[8,4096]{1,0:T(8,128)S(1)}, f32[8,4096]{1,0:T(8,128)}) custom-call(s32[2]{0:T(128)S(1)} %pad_add_fusion.s_ref, f32[8,64,256]{2,1,0:T(8,128)S(1)} %shard_map.70.mine_ref, f32[8,64,256]{2,1,0:T(8,128)S(1)} %collective-permute-done.1.other_ref, f32[8,64]{1,0:T(8,128)S(1)} %get-tuple-element.15.left_ref, ...), custom_call_target="tpu_custom_call" | custom-call | tf_op jit(solution)/shard_map/pallas_call | solution.py:295
  170.0 0.0 reduce-scatter.5.cloned.1.call-done
  170.0 1.6 add_bitcast_fusion
  (7 shorter events, 0.2 us)
Async XLA Ops:
  7.2 82.3 %reduce-scatter.3.cloned.1.call-start = ((), (), s32[]{:S(2)}) async-start(), calls=%async_computation.8 | async-start | bytes 7864320 | tf_op jit(solution)/shard_map/reduce_scatter | solution.py:43
  11.1 66.8 %copy-start = (bf16[1,1,384,4096]{3,2,1,0:T(8,128)(2,1)S(1)}, bf16[1,1,384,4096]{3,2,1,0:T(8,128)(2,1)}, u32[]{:S(2)}) copy-start(bf16[1,1,384,4096]{3,2,1,0:T(8,128)(2,1)} %param.4) | copy-start | bytes 9437188
  11.1 66.8 %copy-start.1 = (f32[1,8,4096]{2,1,0:T(8,128)S(1)}, f32[1,8,4096]{2,1,0:T(8,128)}, u32[]{:S(2)}) copy-start(f32[1,8,4096]{2,1,0:T(8,128)} %param.5) | copy-start | bytes 393220
  62.6 15.3 %all-to-all-start.2 = ((f32[24,8,128]{2,1,0:T(8,128)}), f32[24,8,128]{2,1,0:T(8,128)S(1)}, u32[]{:S(2)}, u32[]{:S(2)}) async-start(f32[24,8,128]{2,1,0:T(8,128)} %broadcast_in_dim.11), calls=%async_computation.2 | async-start | bytes 196608 | tf_op jit(solution)/shard_map/all_to_all | solution.py:35
  66.5 103.6 %reduce-scatter.5.cloned.1.call-start = ((), (), s32[]{:S(2)}) async-start(), calls=%async_computation.9 | async-start | bytes 1703936 | tf_op jit(solution)/shard_map/reduce_scatter | solution.py:43
  80.7 3.8 %collective-permute-start = (f32[8,64,256]{2,1,0:T(8,128)S(1)}, f32[8,64,256]{2,1,0:T(8,128)S(1)}, u32[]{:S(2)}, u32[]{:S(2)}) collective-permute-start(f32[8,64,256]{2,1,0:T(8,128)S(1)} %get-tuple-element.12), channel_id=1, source_target_pairs={{0,48},{48,0},{1,49},{49,1},{2,50},{50,2},{3,51},{51,3},{4,52},{52... | collective-permute-start | bytes 1572872 | tf_op jit(solution)/shard_map/ppermute | solution.py:47
  85.3 4.2 %copy-start.3 = (f32[8,64,256]{2,1,0:T(8,128)S(1)}, f32[8,64,256]{2,1,0:T(8,128)}, u32[]{:S(2)}) copy-start(f32[8,64,256]{2,1,0:T(8,128)} %add.14._) | copy-start | bytes 1572868
  89.5 78.4 %copy-start.2 = (f32[8,4096]{1,0:T(8,128)S(1)}, f32[8,4096]{1,0:T(8,128)}, u32[]{:S(2)}) copy-start(f32[8,4096]{1,0:T(8,128)} %weight_ref.1) | copy-start | bytes 393220
  143.0 20.6 %all-to-all-start.5 = ((f32[32,16,256]{2,1,0:T(8,128)}), f32[32,16,256]{2,1,0:T(8,128)S(1)}, u32[]{:S(2)}, u32[]{:S(2)}) async-start(f32[32,16,256]{2,1,0:T(8,128)} %broadcast_in_dim.13), calls=%async_computation.5 | async-start | bytes 1048576 | tf_op jit(solution)/shard_map/all_to_all | solution.py:35
  164.1 3.8 %collective-permute-start.1 = (f32[8,64,256]{2,1,0:T(8,128)S(1)}, f32[8,64,256]{2,1,0:T(8,128)S(1)}, u32[]{:S(2)}, u32[]{:S(2)}) collective-permute-start(f32[8,64,256]{2,1,0:T(8,128)S(1)} %shard_map.70.mine_ref), channel_id=1, source_target_pairs={{0,48},{48,0},{1,49},{49,1},{2,50},{50,2},{3,51},{51,3},{4,52},{52... | collective-permute-start | bytes 1572872 | tf_op jit(solution)/shard_map/ppermute | solution.py:47
Sparse Core Ops, SparseCore 0:
  11.2 78.2 reduce-scatter.2
  92.6 64.0 reduce-scatter.4
